TPU v7x, 256 devices: a whole 4x4x8 slice. The times are simulated.
256 devices in a mesh: dp: 32 (over z, x), frame: 8 (over y, core).
Axes of the slice: x: 4, y: 4, z: 8, core: 2. Of those that a mesh axis runs over, the one named last changes fastest.
Arguments:
- queries: bfloat16 [32, 2048, 3072], P('dp', 'frame'), may hold values from -68 to 68
- keys: bfloat16 [32, 2048, 3072], P('dp', 'frame'), may hold values from -4 to 4
- values: bfloat16 [32, 2048, 3072], P('dp', 'frame'), may hold values from -5 to 5
- tokens_in: bfloat16 [32, 2048, 3200], P('dp', 'frame'), may hold values from -6 to 6
- out_weight: bfloat16 [3072, 3200], P(None, 'dp'), may hold values from -0.109375 to 0.109375
- pool_keys: bfloat16 [3200, 16], replicated, may hold values from -0.14495689 to 0.14495689
- proj_weight: float32 [3200, 1024], P('frame'), may hold values from -0.109375 to 0.109375
- captions: float32 [32, 1024], P('dp'), may hold values from -6 to 6
- valid_frames: int32 [32], P('dp'), may hold values from 1 to 16, as said below
Outputs:
- block_out: bfloat16 [32, 2048, 3200], P('dp', 'frame')
- clip_loss: float32 [32], P('dp')
Inputs may be any that keep to these rules, and one draw needn't show every extreme that they name: `valid_frames`: every clip has at least one real frame, one clip has all 16, one has a single frame.
All inputs are finite; a program needn't handle non-finite values.
Results may differ from a plain program's by a relative error of at most 0.0029.
Values may be sent and summed in bfloat16 or wider, within the bound.
A program may use at most 128 MiB of HBM per device.

v0:
```python
import jax
import jax.numpy as jnp
from jax import lax
from jax.sharding import PartitionSpec as P

D = 3200
HEADS = 24
HD = 128
G = 16
TPF = 128


sharpness_factor = 1.0 / 0.07


def merged(value, axis, join):
    pieces = jax.tree.map(lambda part: lax.all_gather(part, axis), value)
    head = jax.tree.map(lambda part: part[0], pieces)
    tail = jax.tree.map(lambda part: part[1:], pieces)
    subtotal, _ = lax.scan(lambda subtotal, section: (join(subtotal, section), None), head, tail)
    return subtotal


def attend_heads(head_q, head_k, head_v, keep):
    clip_count, seq_all, heads_here, head_size = head_q.shape
    rows_step = min(512, seq_all)
    key_rows = head_k[0]
    value_rows = head_v[0]
    keep_row = keep[0]

    def one_block(query_block):
        scores = jnp.einsum(
            "qhd,khd->hqk", query_block, key_rows, preferred_element_type=jnp.float32
        )
        scores = scores / jnp.sqrt(jnp.float32(head_size))
        scores = jnp.where(keep_row[None, None, :], scores, jnp.float32(-1e30))
        peak = jnp.max(scores, axis=-1, keepdims=True)
        expo = jnp.exp(scores - peak)
        weights = (expo / jnp.sum(expo, axis=-1, keepdims=True)).astype(jnp.bfloat16)
        return jnp.einsum(
            "hqk,khd->qhd", weights, value_rows, preferred_element_type=jnp.float32
        ).astype(jnp.bfloat16)

    blocks = head_q[0].reshape(seq_all // rows_step, rows_step, heads_here, head_size)
    outputs = [lax.map(one_block, blocks).reshape(seq_all, heads_here, head_size)]
    return jnp.stack(outputs)


def pool_combine(first, second):
    peak = jnp.maximum(first[0], second[0])
    scale_first = jnp.exp(first[0] - peak)
    scale_second = jnp.exp(second[0] - peak)
    total = first[1] * scale_first + second[1] * scale_second
    weighted = first[2] * scale_first[..., None] + second[2] * scale_second[..., None]
    return (peak, total, weighted)


def normalize_rows(matrix):
    return matrix / jnp.sqrt(jnp.sum(matrix * matrix, axis=-1, keepdims=True) + 1e-06)


def local(
    queries, keys, values, tokens_in, out_weight, pool_keys, proj_weight, captions, valid_frames
):
    clip_count, tok_local, width_all = queries.shape
    frame_count = lax.axis_size("frame")
    seq_all = tok_local * frame_count
    frame_index = lax.axis_index("frame")
    shaped_q = queries.reshape(clip_count, tok_local, HEADS, HD)
    shaped_k = keys.reshape(clip_count, tok_local, HEADS, HD)
    shaped_v = values.reshape(clip_count, tok_local, HEADS, HD)
    head_q, head_k, head_v = (
        lax.all_to_all(shaped_q, "frame", split_axis=2, concat_axis=1, tiled=True),
        lax.all_to_all(shaped_k, "frame", split_axis=2, concat_axis=1, tiled=True),
        lax.all_to_all(shaped_v, "frame", split_axis=2, concat_axis=1, tiled=True),
    )
    keep = (jnp.arange(seq_all, dtype=jnp.int32) // TPF)[None, :] < valid_frames[:, None]
    attended = attend_heads(head_q, head_k, head_v, keep)
    back = lax.all_to_all(attended, "frame", split_axis=1, concat_axis=2, tiled=True)
    flat = back.reshape(clip_count * tok_local, width_all)
    projected = jnp.dot(
        flat,
        lax.all_gather(out_weight, "dp", axis=1, tiled=True),
        preferred_element_type=jnp.float32,
    ).reshape(clip_count, tok_local, D)
    block_out = (tokens_in.astype(jnp.float32) + projected).astype(jnp.bfloat16)
    local_ids = frame_index * tok_local + jnp.arange(tok_local, dtype=jnp.int32)
    live = (local_ids // TPF)[None, :] < valid_frames[:, None]
    scores = jnp.einsum("ctd,dg->ctg", block_out, pool_keys, preferred_element_type=jnp.float32)
    masked = jnp.where(live[..., None], scores, jnp.float32(-1e30))
    peak = jnp.max(masked, axis=1)
    expo = jnp.where(live[..., None], jnp.exp(masked - peak[:, None, :]), jnp.float32(0.0))
    total = jnp.sum(expo, axis=1)
    grouped = block_out.astype(jnp.float32).reshape(clip_count, tok_local, G, D // G)
    weighted = jnp.einsum("ctg,ctgd->cgd", expo, grouped, precision=lax.Precision.HIGHEST)
    peak, total, weighted = merged((peak, total, weighted), "frame", pool_combine)
    pooled = (weighted / total[..., None]).reshape(clip_count, D)
    rows_proj = D // frame_count
    pooled_part = lax.dynamic_slice_in_dim(pooled, frame_index * rows_proj, rows_proj, 1)
    partial_emb = jnp.dot(pooled_part, proj_weight, precision=lax.Precision.HIGHEST)
    clip_raw = lax.psum(partial_emb, "frame")
    video_segment_features = normalize_rows(clip_raw)
    sentence_embedding_matrix = normalize_rows(captions)
    aligned_couples = sharpness_factor * jnp.sum(
        video_segment_features * sentence_embedding_matrix, axis=-1
    )
    every_clip, every_caption = (
        lax.all_gather(video_segment_features, "dp", axis=0, tiled=True),
        lax.all_gather(sentence_embedding_matrix, "dp", axis=0, tiled=True),
    )
    per_video_affinity = sharpness_factor * jnp.dot(
        video_segment_features, every_caption.T, precision=lax.Precision.HIGHEST
    )
    per_text_affinity = sharpness_factor * jnp.dot(
        sentence_embedding_matrix, every_clip.T, precision=lax.Precision.HIGHEST
    )
    row_lse = jax.scipy.special.logsumexp(per_video_affinity, axis=1)
    col_lse = jax.scipy.special.logsumexp(per_text_affinity, axis=1)
    clip_loss = 0.5 * (row_lse - aligned_couples) + 0.5 * (col_lse - aligned_couples)
    return (block_out, clip_loss)


def solution(mesh):
    placed = (
        P("dp", "frame", None),
        P("dp", "frame", None),
        P("dp", "frame", None),
        P("dp", "frame", None),
        P(None, "dp"),
        P(),
        P("frame", None),
        P("dp", None),
        P("dp"),
    )
    return jax.shard_map(
        local,
        mesh=mesh,
        in_specs=placed,
        out_specs=(P("dp", "frame", None), P("dp")),
        check_vma=False,
    )
```

profile of v0, /device:TPU:4, one launch (start us, length us, event | category | flops | bytes accessed | tf_op | source)
XLA Modules:
  0.0 384.7 jit_solution(6842300675173830765)
XLA Ops:
  7.2 0.7 all-gather.8.cloned.1.call-update
  7.9 2.6 copy.53
  10.5 4.5 %all-to-all-start = ((bf16[1,256,24,128]{1,3,0,2:T(8,128)(2,1)}), bf16[1,256,24,128]{1,3,0,2:T(8,128)(2,1)S(1)}, u32[]{:S(2)}, u32[]{:S(2)}) async-start(bf16[1,256,24,128]{1,3,0,2:T(8,128)(2,1)} %bitcast.178), calls=%async_computation | async-start | bytes 3145728 | tf_op jit(solution)/shard_map/all_to_all | solution.py:73
  15.0 2.6 copy.57
  17.5 19.0 %all-to-all-done = bf16[1,256,24,128]{1,3,0,2:T(8,128)(2,1)S(1)} async-done(((bf16[1,256,24,128]{1,3,0,2:T(8,128)(2,1)}), bf16[1,256,24,128]{1,3,0,2:T(8,128)(2,1)S(1)}, u32[]{:S(2)}, u32[]{:S(2)}) %all-to-all-start) | async-done | bytes 1572896 | tf_op jit(solution)/shard_map/all_to_all | solution.py:73
  36.5 4.3 %all-to-all-start.1 = ((bf16[1,256,24,128]{1,3,0,2:T(8,128)(2,1)}), bf16[1,256,24,128]{1,3,0,2:T(8,128)(2,1)}, u32[]{:S(2)}, u32[]{:S(2)}) async-start(bf16[1,256,24,128]{1,3,0,2:T(8,128)(2,1)} %bitcast.177), calls=%async_computation.1 | async-start | bytes 3145728 | tf_op jit(solution)/shard_map/all_to_all | solution.py:74
  40.9 2.6 copy.61
  43.5 19.0 %all-to-all-done.1 = bf16[1,256,24,128]{1,3,0,2:T(8,128)(2,1)} async-done(((bf16[1,256,24,128]{1,3,0,2:T(8,128)(2,1)}), bf16[1,256,24,128]{1,3,0,2:T(8,128)(2,1)}, u32[]{:S(2)}, u32[]{:S(2)}) %all-to-all-start.1) | async-done | bytes 1572896 | tf_op jit(solution)/shard_map/all_to_all | solution.py:74
  62.4 4.3 %all-to-all-start.2 = ((bf16[1,256,24,128]{1,3,0,2:T(8,128)(2,1)}), bf16[1,256,24,128]{1,3,0,2:T(8,128)(2,1)}, u32[]{:S(2)}, u32[]{:S(2)}) async-start(bf16[1,256,24,128]{1,3,0,2:T(8,128)(2,1)} %bitcast.176), calls=%async_computation.2 | async-start | bytes 3145728 | tf_op jit(solution)/shard_map/all_to_all | solution.py:75
  66.7 1.6 copy.55
  68.4 3.0 copy.56
  71.4 1.9 copy.59
  73.3 1.2 copy.60
  74.5 13.8 %all-to-all-done.2 = bf16[1,256,24,128]{1,3,0,2:T(8,128)(2,1)} async-done(((bf16[1,256,24,128]{1,3,0,2:T(8,128)(2,1)}), bf16[1,256,24,128]{1,3,0,2:T(8,128)(2,1)}, u32[]{:S(2)}, u32[]{:S(2)}) %all-to-all-start.2) | async-done | bytes 1572896 | tf_op jit(solution)/shard_map/all_to_all | solution.py:75
  88.3 1.9 copy.63
  90.2 1.3 copy.64
  91.5 71.9 %while.26 = (s32[]{:T(128)}, bf16[4,512,3,128]{3,1,0,2:T(8,128)(2,1)}, bf16[4,512,3,128]{3,1,0,2:T(8,128)(2,1)}, bf16[2048,3,128]{2,0,1:T(8,128)(2,1)}, bf16[2048,3,128]{2,0,1:T(8,128)(2,1)}, /*index=5*/s32[]{:T(128)}, s32[]{:T(128)}) while((s32[]{:T(128)}, bf16[4,512,3,128]{3,1,0,2:T(8,128)(2,1)}, ...), condition=%wide.region_3.4_spmd.clone, body=%wide.region_0.3_spmd.clone.sunk | while | flops 1629704192 | bytes 35405948 | solution.py:45
  91.5 0.7 compare_reduce_fusion.2
  92.2 10.2 %fusion.93 = (f32[3,512]{1,0:T(4,128)S(1)}, f32[3,512,2048]{2,1,0:T(8,128)}) fusion(pred[2048]{0:T(1024)(128)(4,1)S(1)} %compare_reduce_fusion.2, bf16[2048,3,128]{2,0,1:T(8,128)(2,1)} %get-tuple-element.305, bf16[4,512,3,128]{3,1,0,2:T(8,128)(2,1)} %get-tuple-element.304, s32[]{:T(128)S(6)} %copy.99), kind=kOutput, calls=%fused_computation.83.clone.1 | convolution fusion | flops 817891328 | bytes 14557188 | tf_op jit(solution)/shard_map/while/body/eval_jaxpr/sub | solution.py:38
  102.4 7.2 %fusion.94 = bf16[4,512,3,128]{3,1,0,2:T(8,128)(2,1)} fusion(bf16[4,512,3,128]{3,1,0,2:T(8,128)(2,1)} %get-tuple-element.296, s32[]{:T(128)S(6)} %copy.99, bf16[2048,3,128]{2,0,1:T(8,128)(2,1)S(1)} %copy-done.2, f32[3,512,2048]{2,1,0:T(8,128)} %get-tuple-element.286, f32[3,512]{1,0:T(4,128)S(1)} %get-tuple-element.287), kind=kOutput, calls=%fused_computation.26.clone.1 | convolution fusion | flops 811794432 | bytes 14555140 | tf_op jit(solution)/shard_map/while/body/eval_jaxpr/hqk,khd->qhd/dot_general | solution.py:40
  109.6 0.7 compare_reduce_fusion.2
  110.3 10.0 %fusion.93 = (f32[3,512]{1,0:T(4,128)S(1)}, f32[3,512,2048]{2,1,0:T(8,128)}) fusion(pred[2048]{0:T(1024)(128)(4,1)S(1)} %compare_reduce_fusion.2, bf16[2048,3,128]{2,0,1:T(8,128)(2,1)} %get-tuple-element.305, bf16[4,512,3,128]{3,1,0,2:T(8,128)(2,1)} %get-tuple-element.304, s32[]{:T(128)S(6)} %copy.99), kind=kOutput, calls=%fused_computation.83.clone.1 | convolution fusion | flops 817891328 | bytes 14557188 | tf_op jit(solution)/shard_map/while/body/eval_jaxpr/sub | solution.py:38
  120.3 7.2 %fusion.94 = bf16[4,512,3,128]{3,1,0,2:T(8,128)(2,1)} fusion(bf16[4,512,3,128]{3,1,0,2:T(8,128)(2,1)} %get-tuple-element.296, s32[]{:T(128)S(6)} %copy.99, bf16[2048,3,128]{2,0,1:T(8,128)(2,1)S(1)} %copy-done.2, f32[3,512,2048]{2,1,0:T(8,128)} %get-tuple-element.286, f32[3,512]{1,0:T(4,128)S(1)} %get-tuple-element.287), kind=kOutput, calls=%fused_computation.26.clone.1 | convolution fusion | flops 811794432 | bytes 14555140 | tf_op jit(solution)/shard_map/while/body/eval_jaxpr/hqk,khd->qhd/dot_general | solution.py:40
  127.5 0.7 compare_reduce_fusion.2
  128.2 10.0 %fusion.93 = (f32[3,512]{1,0:T(4,128)S(1)}, f32[3,512,2048]{2,1,0:T(8,128)}) fusion(pred[2048]{0:T(1024)(128)(4,1)S(1)} %compare_reduce_fusion.2, bf16[2048,3,128]{2,0,1:T(8,128)(2,1)} %get-tuple-element.305, bf16[4,512,3,128]{3,1,0,2:T(8,128)(2,1)} %get-tuple-element.304, s32[]{:T(128)S(6)} %copy.99), kind=kOutput, calls=%fused_computation.83.clone.1 | convolution fusion | flops 817891328 | bytes 14557188 | tf_op jit(solution)/shard_map/while/body/eval_jaxpr/sub | solution.py:38
  138.1 7.3 %fusion.94 = bf16[4,512,3,128]{3,1,0,2:T(8,128)(2,1)} fusion(bf16[4,512,3,128]{3,1,0,2:T(8,128)(2,1)} %get-tuple-element.296, s32[]{:T(128)S(6)} %copy.99, bf16[2048,3,128]{2,0,1:T(8,128)(2,1)S(1)} %copy-done.2, f32[3,512,2048]{2,1,0:T(8,128)} %get-tuple-element.286, f32[3,512]{1,0:T(4,128)S(1)} %get-tuple-element.287), kind=kOutput, calls=%fused_computation.26.clone.1 | convolution fusion | flops 811794432 | bytes 14555140 | tf_op jit(solution)/shard_map/while/body/eval_jaxpr/hqk,khd->qhd/dot_general | solution.py:40
  145.4 0.7 compare_reduce_fusion.2
  146.1 10.0 %fusion.93 = (f32[3,512]{1,0:T(4,128)S(1)}, f32[3,512,2048]{2,1,0:T(8,128)}) fusion(pred[2048]{0:T(1024)(128)(4,1)S(1)} %compare_reduce_fusion.2, bf16[2048,3,128]{2,0,1:T(8,128)(2,1)} %get-tuple-element.305, bf16[4,512,3,128]{3,1,0,2:T(8,128)(2,1)} %get-tuple-element.304, s32[]{:T(128)S(6)} %copy.99), kind=kOutput, calls=%fused_computation.83.clone.1 | convolution fusion | flops 817891328 | bytes 14557188 | tf_op jit(solution)/shard_map/while/body/eval_jaxpr/sub | solution.py:38
  156.1 7.3 %fusion.94 = bf16[4,512,3,128]{3,1,0,2:T(8,128)(2,1)} fusion(bf16[4,512,3,128]{3,1,0,2:T(8,128)(2,1)} %get-tuple-element.296, s32[]{:T(128)S(6)} %copy.99, bf16[2048,3,128]{2,0,1:T(8,128)(2,1)S(1)} %copy-done.2, f32[3,512,2048]{2,1,0:T(8,128)} %get-tuple-element.286, f32[3,512]{1,0:T(4,128)S(1)} %get-tuple-element.287), kind=kOutput, calls=%fused_computation.26.clone.1 | convolution fusion | flops 811794432 | bytes 14555140 | tf_op jit(solution)/shard_map/while/body/eval_jaxpr/hqk,khd->qhd/dot_general | solution.py:40
  163.4 4.1 %copy.67 = bf16[1,2048,3,128]{3,2,0,1:T(4,128)(2,1)} copy(bf16[1,2048,3,128]{3,1,2,0:T(8,128)(2,1)} %bitcast.183) | data formatting | bytes 3145728 | tf_op jit(solution)/shard_map/stack;reshape | solution.py:46
  167.6 4.7 %all-to-all-start.3 = ((bf16[1,2048,3,128]{3,2,0,1:T(4,128)(2,1)}), bf16[1,2048,3,128]{3,2,0,1:T(4,128)(2,1)}, u32[]{:S(2)}, u32[]{:S(2)}) async-start(bf16[1,2048,3,128]{3,2,0,1:T(4,128)(2,1)} %copy.67), calls=%async_computation.3 | async-start | bytes 4194304 | tf_op jit(solution)/shard_map/all_to_all | solution.py:79
  175.4 23.9 %all-to-all-done.3 = bf16[1,2048,3,128]{3,2,0,1:T(4,128)(2,1)} async-done(((bf16[1,2048,3,128]{3,2,0,1:T(4,128)(2,1)}), bf16[1,2048,3,128]{3,2,0,1:T(4,128)(2,1)}, u32[]{:S(2)}, u32[]{:S(2)}) %all-to-all-start.3) | async-done | bytes 1572896 | tf_op jit(solution)/shard_map/all_to_all | solution.py:79
  199.2 1.8 copy.68
  201.1 1.6 copy.69
  202.6 20.3 %reshape.245 = bf16[3200,3072]{1,0:T(8,128)(2,1)} reshape(bf16[32,100,3072]{2,1,0:T(8,128)(2,1)} %all-gather.8.cloned.1.call-done) | data formatting | bytes 39321600
  222.9 10.8 %fusion.39 = bf16[1,256,3200]{2,1,0:T(8,128)(2,1)S(1)} fusion(bf16[256,3072]{0,1:T(8,128)(2,1)} %bitcast.187, bf16[3200,3072]{1,0:T(8,128)(2,1)} %reshape.245, bf16[1,256,3200]{2,1,0:T(8,128)(2,1)} %param.16), kind=kOutput, calls=%fused_computation.43 | convolution fusion | flops 5035622400 | bytes 24510464 | tf_op jit(solution)/shard_map/dot_general | solution.py:81
  233.7 0.7 fusion.68
  235.1 12.8 %all-reduce.2 = (f32[128]{0:T(128)S(1)}, f32[128]{0:T(128)S(1)}) all-reduce(f32[128]{0:T(128)S(1)} %dynamic-update-slice, f32[128]{0:T(128)S(1)} %dynamic-update-slice.1), channel_id=2, replica_groups=mesh['dp'=32,'frame'=8] {'frame'}, use_global_device_ids=true, to_apply=%add | all-reduce | flops 256 | bytes 2048
  248.0 2.2 copy.70
  250.2 2.8 fusion.51
  253.0 12.8 %all-gather.2 = f32[128,200]{1,0:T(8,128)S(1)} all-gather(f32[16,200]{1,0:T(8,128)S(1)} %bitcast.190), channel_id=4, replica_groups=mesh['dp'=32,'frame'=8] {'frame'}, dimensions={0}, use_global_device_ids=true | all-gather | bytes 115200 | tf_op jit(solution)/shard_map/all_gather | solution.py:17
  266.0 0.8 while.25
  267.0 0.9 fusion.57
  267.9 12.7 %psum.7 = f32[1,1024]{1,0:T(1,128)S(1)} all-reduce(f32[1,1024]{1,0:T(1,128)S(1)} %fusion.57), channel_id=1, replica_groups=mesh['dp'=32,'frame'=8] {'frame'}, use_global_device_ids=true, to_apply=%region_8.9 | all-reduce | flops 1024 | bytes 8192 | tf_op jit(solution)/shard_map/psum | solution.py:101
  282.5 45.0 %all-gather.4 = f32[32,1,1024]{2,1,0:T(1,128)S(1)} all-gather(f32[1,1,1024]{2,1,0:T(1,128)S(1)} %bitcast.191), channel_id=1, replica_groups=mesh['dp'=32,'frame'=8] {'dp'}, dimensions={0}, use_global_device_ids=true | all-gather | bytes 135168 | tf_op jit(solution)/shard_map/all_gather | solution.py:109
  327.5 0.8 fusion.69
  330.7 42.2 %all-gather.5 = f32[32,1,1024]{2,1,0:T(1,128)S(1)} all-gather(f32[1,1,1024]{2,1,0:T(1,128)S(1)} %bitcast.192), channel_id=1, replica_groups=mesh['dp'=32,'frame'=8] {'dp'}, dimensions={0}, use_global_device_ids=true | all-gather | bytes 135168 | tf_op jit(solution)/shard_map/all_gather | solution.py:108
  372.9 0.8 fusion.70
  (71 shorter events, 5.6 us)
Async XLA Ops:
  7.2 259.8 %copy-start = (f32[400,1024]{1,0:T(8,128)S(1)}, f32[400,1024]{1,0:T(8,128)}, u32[]{:S(2)}) copy-start(f32[400,1024]{1,0:T(8,128)} %param.19) | copy-start | bytes 4915204
  7.2 195.4 %all-gather.8.cloned.1.call-start = ((), (), s32[]{:S(2)}) async-start(), calls=%async_computation.4 | async-start | bytes 21086208 | tf_op jit(solution)/shard_map/all_gather | solution.py:83
  10.5 26.1 %all-to-all-start = ((bf16[1,256,24,128]{1,3,0,2:T(8,128)(2,1)}), bf16[1,256,24,128]{1,3,0,2:T(8,128)(2,1)S(1)}, u32[]{:S(2)}, u32[]{:S(2)}) async-start(bf16[1,256,24,128]{1,3,0,2:T(8,128)(2,1)} %bitcast.178), calls=%async_computation | async-start | bytes 3145728 | tf_op jit(solution)/shard_map/all_to_all | solution.py:73
  36.5 25.9 %all-to-all-start.1 = ((bf16[1,256,24,128]{1,3,0,2:T(8,128)(2,1)}), bf16[1,256,24,128]{1,3,0,2:T(8,128)(2,1)}, u32[]{:S(2)}, u32[]{:S(2)}) async-start(bf16[1,256,24,128]{1,3,0,2:T(8,128)(2,1)} %bitcast.177), calls=%async_computation.1 | async-start | bytes 3145728 | tf_op jit(solution)/shard_map/all_to_all | solution.py:74
  62.4 25.9 %all-to-all-start.2 = ((bf16[1,256,24,128]{1,3,0,2:T(8,128)(2,1)}), bf16[1,256,24,128]{1,3,0,2:T(8,128)(2,1)}, u32[]{:S(2)}, u32[]{:S(2)}) async-start(bf16[1,256,24,128]{1,3,0,2:T(8,128)(2,1)} %bitcast.176), calls=%async_computation.2 | async-start | bytes 3145728 | tf_op jit(solution)/shard_map/all_to_all | solution.py:75
  92.2 10.2 %copy-start.2 = (bf16[2048,3,128]{2,0,1:T(8,128)(2,1)S(1)}, bf16[2048,3,128]{2,0,1:T(8,128)(2,1)}, u32[]{:S(2)}) copy-start(bf16[2048,3,128]{2,0,1:T(8,128)(2,1)} %get-tuple-element.306) | copy-start | bytes 4718596 | tf_op jit(solution)/shard_map/while
  110.3 10.0 %copy-start.2 = (bf16[2048,3,128]{2,0,1:T(8,128)(2,1)S(1)}, bf16[2048,3,128]{2,0,1:T(8,128)(2,1)}, u32[]{:S(2)}) copy-start(bf16[2048,3,128]{2,0,1:T(8,128)(2,1)} %get-tuple-element.306) | copy-start | bytes 4718596 | tf_op jit(solution)/shard_map/while
  128.2 10.0 %copy-start.2 = (bf16[2048,3,128]{2,0,1:T(8,128)(2,1)S(1)}, bf16[2048,3,128]{2,0,1:T(8,128)(2,1)}, u32[]{:S(2)}) copy-start(bf16[2048,3,128]{2,0,1:T(8,128)(2,1)} %get-tuple-element.306) | copy-start | bytes 4718596 | tf_op jit(solution)/shard_map/while
  146.1 10.0 %copy-start.2 = (bf16[2048,3,128]{2,0,1:T(8,128)(2,1)S(1)}, bf16[2048,3,128]{2,0,1:T(8,128)(2,1)}, u32[]{:S(2)}) copy-start(bf16[2048,3,128]{2,0,1:T(8,128)(2,1)} %get-tuple-element.306) | copy-start | bytes 4718596 | tf_op jit(solution)/shard_map/while
  167.5 5.3 %copy-start.4 = (f32[1,1024]{1,0:T(1,128)S(1)}, f32[1,1024]{1,0:T(1,128)}, u32[]{:S(2)}) copy-start(f32[1,1024]{1,0:T(1,128)} %param.20) | copy-start | bytes 12292
  167.5 6.6 %copy-start.5 = (u32[256]{0:T(256)S(1)}, u32[256]{0:T(256)}, u32[]{:S(2)}) copy-start(u32[256]{0:T(256)} %constant.96) | copy-start | bytes 3076
  167.6 31.7 %all-to-all-start.3 = ((bf16[1,2048,3,128]{3,2,0,1:T(4,128)(2,1)}), bf16[1,2048,3,128]{3,2,0,1:T(4,128)(2,1)}, u32[]{:S(2)}, u32[]{:S(2)}) async-start(bf16[1,2048,3,128]{3,2,0,1:T(4,128)(2,1)} %copy.67), calls=%async_computation.3 | async-start | bytes 4194304 | tf_op jit(solution)/shard_map/all_to_all | solution.py:79
  222.9 10.8 %copy-start.3 = (bf16[3200,16]{0,1:T(8,128)(2,1)S(1)}, bf16[3200,16]{0,1:T(8,128)(2,1)}, u32[]{:S(2)}) copy-start(bf16[3200,16]{0,1:T(8,128)(2,1)} %param.18) | copy-start | bytes 307204
  233.7 16.5 %copy-start.1 = (bf16[1,256,3200]{2,1,0:T(8,128)(2,1)}, bf16[1,256,3200]{2,1,0:T(8,128)(2,1)S(1)}, u32[]{:S(2)}) copy-start(bf16[1,256,3200]{2,1,0:T(8,128)(2,1)S(1)} %fusion.39) | copy-start | bytes 4915204
Sparse Core Ops, SparseCore 0:
  10.6 159.7 all-gather.7
where the time goes:
time: 386 us; the launch traced here: 385 us
  blocking collectives  125 us (32%)
  matrix products  85.8 us (22%)
  waiting for transfers between devices  76.3 us (20%)
  local copies, waits for them, and re-layouts  50.4 us (13%)
  between operations  22 us (6%)
  starting transfers between devices  17.8 us (5%)
  other arithmetic  6.79 us (2%)
    all_gather x1, blocking collectives, local(): lax.all_gather(sentence_embedding_matrix, 'dp', axis=0, tiled=True)  45 us
    all_gather x1, blocking collectives, local(): lax.all_gather(video_segment_features, 'dp', axis=0, tiled=True)  42.2 us
    sub x4, matrix products, one_block(): expo = jnp.exp(scores - peak)  40.1 us
    unnamed x19, local copies, waits for them, and re-layouts  29.1 us
    dot_general x4, matrix products, one_block(): jnp.einsum('hqk,khd->qhd', weights, value_rows, preferred_element_type=jn...  29 us
    all_to_all x1, waiting for transfers between devices, local(): lax.all_to_all(attended, 'frame', split_axis=1, concat_axis=2, tiled=True)  23.9 us
    all_to_all x1, waiting for transfers between devices, local(): lax.all_to_all(shaped_q, 'frame', split_axis=2, concat_axis=1, tiled=True)  19 us
    all_to_all x1, waiting for transfers between devices, local(): lax.all_to_all(shaped_k, 'frame', split_axis=2, concat_axis=1, tiled=True)  19 us
  transfers between devices with their start and end apart: 5, of which 4 were waited for; matrix products, arithmetic and copies ran while one was open for 26% of the time, Pallas kernels for 0%

commit v1 on v0

v1 whole, which is shorter than its diff:
```python
import functools

import jax
import jax.numpy as jnp
from jax import lax
from jax.experimental import pallas as pl
from jax.experimental.pallas import tpu as pltpu
from jax.sharding import PartitionSpec as P

D = 3200
HEADS = 24
HD = 128
G = 16
TPF = 128
SEQ = 2048
TOK = 256
ROUNDS = 3
NF = 8
NZ = 8
NX = 4
KR = NF * HD
PIECE = 100
PAD = 128
WIDE = NZ * NX * PAD
XPART = 224
ZPART = 288
SCALE = 1.4426950408889634 / (128.0**0.5)
SHARP = 1.0 / 0.07

MESH = pl.DeviceIdType.MESH
F32 = jnp.float32
BF16 = jnp.bfloat16


def nt_dot(a, b):
    return lax.dot_general(a, b, (((1,), (1,)), ((), ())), preferred_element_type=F32)


def body(
    q_hbm, k_hbm, v_hbm, tok_hbm, w_hbm, pk_ref, proj_hbm, cap_ref, valid_ref,
    out_hbm, loss_ref,
    tok, wown, proj, projp, wbuf, qkv, k2, vext, osend, orecv, acc, blk, outv,
    msg, parts, emb, embs, caps, logit,
    lsem, qs, qr, os_, or_, z1s, z1r, z2s, z2r, x1s, x1r, x2s, x2r, sbs, sbr,
    cs, cr, ms, mr, es, er, gs, gr,
):
    dp = lax.axis_index("dp")
    f = lax.axis_index("frame")
    z = dp // NX
    x = lax.rem(dp, NX)
    c = lax.rem(f, 2)
    sib = f + 1 - 2 * c
    sign = 1 - 2 * c
    valid = valid_ref[0]

    def at_z(zz):
        return {"dp": zz * NX + x}

    def at_x(xx):
        return {"dp": z * NX + xx}

    def remote(src, dst, ssem, rsem, where):
        return pltpu.make_async_remote_copy(
            src_ref=src, dst_ref=dst, send_sem=ssem, recv_sem=rsem, device_id=where, device_id_type=MESH
        )

    loads = [
        pltpu.make_async_copy(w_hbm, wown, lsem.at[0]),
        pltpu.make_async_copy(tok_hbm, tok, lsem.at[1]),
        pltpu.make_async_copy(proj_hbm, proj, lsem.at[2]),
    ]
    for load in loads:
        load.start()

    barrier = pltpu.get_barrier_semaphore()
    for i in range(1, NF):
        pl.semaphore_signal(barrier, inc=1, device_id={"frame": lax.rem(f + i, NF)}, device_id_type=MESH)
    for i in range(1, NX):
        pl.semaphore_signal(barrier, inc=1, device_id=at_x(lax.rem(x + i, NX)), device_id_type=MESH)
    for i in range(1, NZ):
        pl.semaphore_signal(barrier, inc=1, device_id=at_z(lax.rem(z + i, NZ)), device_id_type=MESH)

    loads[0].wait()
    for r in range(ROUNDS):
        rows = pl.ds(pl.multiple_of(r * KR + c * 512, 512), 512)
        wbuf[z, x, rows, :] = jnp.zeros((512, PAD), BF16)
        wbuf[z, x, rows, 0:PIECE] = wown[rows, :]
    pl.semaphore_wait(barrier, NF - 1 + NX - 1 + NZ - 1)

    def xrows(r, core):
        return pl.ds(pl.multiple_of(r * KR + core * 512, 16), XPART)

    def zrows(r, core):
        return pl.ds(pl.multiple_of(r * KR + core * 512 + XPART, 16), ZPART)

    sends = []

    def go(copy):
        copy.start()
        sends.append(copy)

    def zturn(way, step):
        s = sign if way == 0 else -sign
        return lax.rem(z - s * step + NZ, NZ)

    def znext(way):
        s = sign if way == 0 else -sign
        return lax.rem(z + s + NZ, NZ)

    LAST = (4, 3)

    def z2_block(r, zb):
        return wbuf.at[zb, x, zrows(r, c), :]

    def z1_block(r, zb):
        return wbuf.at[zb, :, xrows(r, c), :]

    def z_copy(block, r, way, step, ss, rs):
        ref = block(r, zturn(way, step))
        return remote(ref, ref, ss.at[r, way, step], rs.at[r, way, step], at_z(znext(way)))

    def z_send(block, r, step, ss, rs):
        for way in range(2):
            if step < LAST[way]:
                go(z_copy(block, r, way, step, ss, rs))

    def z_step(block, r, step, ss, rs):
        for way in range(2):
            if step <= LAST[way]:
                ref = block(r, zturn(way, step))
                remote(ref, ref, ss.at[r, way, step - 1], rs.at[r, way, step - 1], at_z(znext(way))).wait_recv()
                if step < LAST[way]:
                    go(z_copy(block, r, way, step, ss, rs))

    def z2_start(r):
        z_send(z2_block, r, 0, z2s, z2r)

    def z2_step(r, step):
        z_step(z2_block, r, step, z2s, z2r)

    def z1_start(r):
        z_send(z1_block, r, 0, z1s, z1r)

    def z1_step(r, step):
        z_step(z1_block, r, step, z1s, z1r)

    def x1_copy(r, i, xx):
        ref = wbuf.at[z, xx, xrows(r, c), :]
        return remote(ref, ref, x1s.at[r, i - 1], x1r.at[r, i - 1], at_x(lax.rem(x + i, NX)))

    def x1_start(r):
        for i in range(1, NX):
            go(x1_copy(r, i, x))

    def x1_wait(r):
        for i in range(1, NX):
            x1_copy(r, i, lax.rem(x - i + NX, NX)).wait_recv()

    right = lax.rem(x + 1, NX)
    left = lax.rem(x + NX - 1, NX)
    across = lax.rem(x + 2, NX)

    def x2_copy(r, which, xx):
        part = (pl.ds(0, NZ), pl.ds(0, NZ), pl.ds(0, 4), pl.ds(4, 4))[which]
        ref = wbuf.at[part, xx, zrows(r, c), :]
        to = (right, left, right, left)[which]
        return remote(ref, ref, x2s.at[r, which], x2r.at[r, which], at_x(to))

    def x2_start(r):
        go(x2_copy(r, 0, x))
        go(x2_copy(r, 1, x))

    def x2_forward(r):
        x2_copy(r, 0, left).wait_recv()
        go(x2_copy(r, 2, left))
        x2_copy(r, 1, right).wait_recv()
        go(x2_copy(r, 3, right))

    def x2_finish(r):
        x2_copy(r, 2, across).wait_recv()
        x2_copy(r, 3, across).wait_recv()

    def sib_copy(r, which, core):
        ref = wbuf.at[:, :, (xrows, zrows)[which](r, core), :]
        return remote(ref, ref, sbs.at[r, which], sbr.at[r, which], {"frame": sib})

    def sib_start(r, which):
        go(sib_copy(r, which, c))

    def sib_wait(r):
        for which in range(2):
            sib_copy(r, which, 1 - c).wait_recv()

    def qkv_start(r):
        for i in range(1, NF):
            t = lax.rem(f + i, NF)
            cols = pl.ds(pl.multiple_of((r * NF + t) * HD, HD), HD)
            for a, ref in enumerate((k_hbm, v_hbm, q_hbm)):
                remote(
                    ref.at[:, cols],
                    qkv.at[r, a, pl.ds(pl.multiple_of(f * TOK, TOK), TOK), :],
                    qs.at[r], qr.at[r], {"frame": t},
                ).start()
        cols = pl.ds(pl.multiple_of((r * NF + f) * HD, HD), HD)
        for a, ref in enumerate((k_hbm, v_hbm, q_hbm)):
            pltpu.make_async_copy(
                ref.at[:, cols], qkv.at[r, a, pl.ds(pl.multiple_of(f * TOK, TOK), TOK), :], qr.at[r]
            ).start()

    def qkv_wait(r):
        pltpu.make_async_copy(qkv.at[r], qkv.at[r], qr.at[r]).wait()

    def attend(r):
        qkv_wait(r)
        for i in range(8):
            rows = slice(256 * i, 256 * (i + 1))
            live = (lax.broadcasted_iota(jnp.int32, (256, HD), 0) + 256 * i) // TPF < valid
            kk = qkv[r, 0, rows, :].astype(F32)
            first = qkv[r, 0, 0:16, :].astype(F32)[0:1, :]
            kk = jnp.where(live, kk, jnp.broadcast_to(first, (256, HD))) * SCALE
            hi = kk.astype(BF16)
            k2[rows, 0:HD] = hi
            k2[rows, HD : 2 * HD] = (kk - hi.astype(F32)).astype(BF16)
            vext[rows, 0:HD] = jnp.where(live, qkv[r, 1, rows, :].astype(F32), 0.0).astype(BF16)
            vext[rows, HD : 2 * HD] = jnp.where(live, 1.0, 0.0).astype(BF16)

        def block(i, carry):
            b = lax.rem(f + 1 + i, NF)
            qq = qkv[r, 2, pl.ds(pl.multiple_of(b * TOK, TOK), TOK), :]
            scores = nt_dot(jnp.concatenate([qq, qq], axis=1), k2[...])
            peak = jnp.max(scores, axis=1, keepdims=True)
            weights = jnp.exp2(scores - peak).astype(BF16)
            both = jnp.dot(weights, vext[...], preferred_element_type=F32)
            osend[r, b] = (both[:, 0:HD] / both[:, HD : 2 * HD]).astype(BF16)
            cols = pl.ds(pl.multiple_of(r * KR + f * HD, HD), HD)

            @pl.when(i < NF - 1)
            def _():
                remote(osend.at[r, b], orecv.at[:, cols], os_.at[r], or_.at[r], {"frame": b}).start()

            @pl.when(i == NF - 1)
            def _():
                pltpu.make_async_copy(osend.at[r, b], orecv.at[:, cols], or_.at[r]).start()

            return carry

        lax.fori_loop(0, NF, block, 0)

    def attended_wait(r):
        cols = orecv.at[:, pl.ds(r * KR, KR)]
        pltpu.make_async_copy(cols, cols, or_.at[r]).wait()

    def project(r):
        def step(zz, carry):
            for pair in range(2):
                rows = pl.ds(r * KR, KR)
                rhs = jnp.concatenate([wbuf[zz, 2 * pair, rows, :], wbuf[zz, 2 * pair + 1, rows, :]], axis=1)
                cols = pl.ds(pl.multiple_of(zz * 512 + pair * 256, 256), 256)
                total = acc[:, cols] + jnp.dot(
                    orecv[:, r * KR : (r + 1) * KR], rhs, preferred_element_type=F32
                )
                if r < ROUNDS - 1:
                    acc[:, cols] = total
                else:
                    blk[:, cols] = total.astype(BF16)
            return carry

        lax.fori_loop(0, NZ, step, 0)

    for r in range(ROUNDS):
        z2_start(r)
        x1_start(r)
        qkv_start(r)

    for n in range(8):
        emb[0, n : n + 1, :] = cap_ref[0:1, 128 * n : 128 * (n + 1)]
    own_cap = emb[0]
    norm = jnp.sqrt(jnp.sum(own_cap * own_cap, keepdims=True) + 1e-06)
    caps[z, x] = own_cap / norm
    cap_sends = []

    def cap_x(i, xx):
        ref = caps.at[z, xx]
        return remote(ref, ref, cs.at[i - 1], cr.at[i - 1], at_x(lax.rem(x + i, NX)))

    def cap_z(i, zz):
        ref = caps.at[zz]
        return remote(ref, ref, cs.at[NX - 2 + i], cr.at[NX - 2 + i], at_z(lax.rem(z + i, NZ)))

    for i in range(1, NX):
        go(cap_x(i, x))

    loads[1].wait()
    for j in range(NZ * NX):
        acc[:, PAD * j : PAD * (j + 1)] = jnp.zeros((TOK, PAD), F32)
        acc[:, PAD * j : PAD * j + PIECE] = tok[:, PIECE * j : PIECE * (j + 1)].astype(F32)

    for step in range(1, 5):
        z2_step(0, step)
    x2_start(0)
    x1_wait(0)
    z1_start(0)

    for i in range(1, NX):
        cap_x(i, lax.rem(x - i + NX, NX)).wait_recv()
    for i in range(1, NZ):
        go(cap_z(i, z))

    loads[2].wait()
    projp[...] = jnp.zeros((512, 1024), F32)
    for i in range(4):
        projp[PAD * i : PAD * i + PIECE, :] = proj[PIECE * i : PIECE * (i + 1), :]

    for step in range(1, 5):
        z2_step(1, step)
    x2_forward(0)
    x2_start(1)
    for step in range(1, 5):
        z1_step(0, step)
    x1_wait(1)
    z1_start(1)

    attend(0)

    sib_start(0, 0)
    x2_finish(0)
    sib_start(0, 1)
    for step in range(1, 5):
        z2_step(2, step)
    x2_forward(1)
    x2_start(2)
    for step in range(1, 5):
        z1_step(1, step)
    x1_wait(2)
    z1_start(2)

    attend(1)

    sib_start(1, 0)
    x2_finish(1)
    sib_start(1, 1)

    attend(2)

    sib_wait(0)
    attended_wait(0)
    project(0)
    x2_forward(2)
    for step in range(1, 5):
        z1_step(2, step)
    sib_start(2, 0)
    sib_wait(1)
    attended_wait(1)
    project(1)
    x2_finish(2)
    sib_start(2, 1)
    for i in range(1, NZ):
        cap_z(i, lax.rem(z - i + NZ, NZ)).wait_recv()
    sib_wait(2)
    attended_wait(2)
    project(2)

    scores = nt_dot(pk_ref[...], blk[...])
    token = lax.broadcasted_iota(jnp.int32, (G, TOK), 1) + f * TOK
    live = token // TPF < valid
    masked = jnp.where(live, scores, -1e30)
    peak = jnp.max(masked, axis=1, keepdims=True)
    expo = jnp.where(live, jnp.exp(masked - peak), 0.0)
    total = jnp.sum(expo, axis=1, keepdims=True)
    e0 = expo.astype(BF16)
    rest = expo - e0.astype(F32)
    e1 = rest.astype(BF16)
    e2 = (rest - e1.astype(F32)).astype(BF16)
    w48 = jnp.dot(jnp.concatenate([e0, e1, e2], axis=0), blk[...], preferred_element_type=F32)
    w16 = w48[0:G] + w48[G : 2 * G] + w48[2 * G : 3 * G]
    mine = lax.broadcasted_iota(jnp.int32, (G, WIDE), 1) // (2 * PAD) == lax.broadcasted_iota(jnp.int32, (G, WIDE), 0)

    def spread(value):
        return jnp.sum(jnp.where(mine, value, 0.0), axis=0, keepdims=True)

    msg[0:1, :] = spread(w16)
    msg[1:2, :] = spread(jnp.broadcast_to(peak, (G, WIDE)))
    msg[2:3, :] = spread(jnp.broadcast_to(total, (G, WIDE)))
    msg[3:8, :] = jnp.zeros((5, WIDE), F32)

    def part_copy(i, src):
        t = lax.rem(f + i, NF)
        return remote(
            msg.at[:, pl.ds(pl.multiple_of(t * 512, 512), 512)], parts.at[src],
            ms.at[i - 1], mr.at[i - 1], {"frame": t},
        )

    for i in range(1, NF):
        go(part_copy(i, f))
    parts[f] = msg[:, pl.ds(pl.multiple_of(f * 512, 512), 512)]

    for j in range(NZ * NX):
        outv[:, PIECE * j : PIECE * (j + 1)] = blk[:, PAD * j : PAD * j + PIECE]
    store = pltpu.make_async_copy(outv, out_hbm, lsem.at[0])
    store.start()

    for i in range(1, NF):
        part_copy(i, lax.rem(f - i + NF, NF)).wait_recv()
    gathered = parts[...]
    peaks = gathered[:, 1, :]
    top = jnp.max(peaks, axis=0, keepdims=True)
    scale = jnp.exp(peaks - top)
    denominator = jnp.sum(gathered[:, 2, :] * scale, axis=0, keepdims=True)
    pooled = jnp.sum(gathered[:, 0, :] * scale, axis=0, keepdims=True) / denominator
    column = jnp.transpose(jnp.broadcast_to(pooled, (PAD, 512)))
    for n in range(8):
        emb[0, n : n + 1, :] = jnp.sum(column * projp[:, 128 * n : 128 * (n + 1)], axis=0, keepdims=True)

    def emb_copy(i, src):
        return remote(emb.at[0], embs.at[src], es.at[i - 1], er.at[i - 1], {"frame": lax.rem(f + i, NF)})

    for i in range(1, NF):
        go(emb_copy(i, f))
    embs[f] = emb[0]
    for i in range(1, NF):
        emb_copy(i, lax.rem(f - i + NF, NF)).wait_recv()
    raw = jnp.sum(embs[...], axis=0)
    clip = raw / jnp.sqrt(jnp.sum(raw * raw, keepdims=True) + 1e-06)

    products = jnp.sum(caps[...].reshape(NZ * NX, 8, 128) * clip[None], axis=1)
    square = jnp.concatenate([products, jnp.zeros((96, 128), F32)], axis=0)
    row = SHARP * jnp.sum(jnp.transpose(square), axis=0, keepdims=True)
    logit[z, x] = jnp.broadcast_to(row, (8, 128))

    def log_x(i, xx):
        ref = logit.at[z, xx]
        return remote(ref, ref, gs.at[i - 1], gr.at[i - 1], at_x(lax.rem(x + i, NX)))

    def log_z(i, zz):
        ref = logit.at[zz]
        return remote(ref, ref, gs.at[NX - 2 + i], gr.at[NX - 2 + i], at_z(lax.rem(z + i, NZ)))

    for i in range(1, NX):
        go(log_x(i, x))
    lane = lax.broadcasted_iota(jnp.int32, (1, 128), 1)
    own = jnp.where(lane < NZ * NX, row, -jnp.inf)
    own_top = jnp.max(own, axis=1, keepdims=True)
    row_lse = jnp.log(jnp.sum(jnp.exp(own - own_top), axis=1, keepdims=True)) + own_top
    for i in range(1, NX):
        log_x(i, lax.rem(x - i + NX, NX)).wait_recv()
    for i in range(1, NZ):
        go(log_z(i, z))
    for i in range(1, NZ):
        log_z(i, lax.rem(z - i + NZ, NZ)).wait_recv()
    table = logit[...].reshape(NZ * NX, 8, 128)
    col_top = jnp.max(table, axis=0)
    col_lse = (jnp.log(jnp.sum(jnp.exp(table - col_top[None]), axis=0)) + col_top)[0:1, :]
    picked = jnp.where(lane == dp, 0.5 * col_lse - row, 0.0)
    value = 0.5 * row_lse + jnp.sum(picked, axis=1, keepdims=True)
    loss_ref[...] = jnp.broadcast_to(value, (1, 128))

    for copy in sends:
        copy.wait_send()
    for r in range(ROUNDS):
        away = qkv.at[r, :, pl.ds(0, SEQ - TOK), :]
        pltpu.make_async_copy(away, away, qs.at[r]).wait()
        away = orecv.at[:, pl.ds(0, KR - HD)]
        pltpu.make_async_copy(away, away, os_.at[r]).wait()
    store.wait()


def local(
    queries, keys, values, tokens_in, out_weight, pool_keys, proj_weight, captions, valid_frames
):
    pool = jnp.pad(pool_keys.reshape(NZ * NX, PIECE, G), ((0, 0), (0, PAD - PIECE), (0, 0))).reshape(WIDE, G).T
    any_ = pl.BlockSpec(memory_space=pl.ANY)
    vmem = pl.BlockSpec(memory_space=pltpu.VMEM)
    smem = pl.BlockSpec(memory_space=pltpu.SMEM)
    dma = pltpu.SemaphoreType.DMA
    block_out, loss = pl.pallas_call(
        body,
        out_shape=(
            jax.ShapeDtypeStruct((TOK, D), BF16),
            jax.ShapeDtypeStruct((1, 128), F32),
        ),
        in_specs=[any_, any_, any_, any_, any_, vmem, any_, vmem, smem],
        out_specs=(any_, vmem),
        scratch_shapes=[
            pltpu.VMEM((TOK, D), BF16),
            pltpu.VMEM((HEADS * HD, PIECE), BF16),
            pltpu.VMEM((400, 1024), F32),
            pltpu.VMEM((512, 1024), F32),
            pltpu.VMEM((NZ, NX, HEADS * HD, PAD), BF16),
            pltpu.VMEM((ROUNDS, 3, SEQ, HD), BF16),
            pltpu.VMEM((SEQ, 2 * HD), BF16),
            pltpu.VMEM((SEQ, 2 * HD), BF16),
            pltpu.VMEM((ROUNDS, NF, TOK, HD), BF16),
            pltpu.VMEM((TOK, HEADS * HD), BF16),
            pltpu.VMEM((TOK, WIDE), F32),
            pltpu.VMEM((TOK, WIDE), BF16),
            pltpu.VMEM((TOK, D), BF16),
            pltpu.VMEM((8, WIDE), F32),
            pltpu.VMEM((NF, 8, 512), F32),
            pltpu.VMEM((1, 8, 128), F32),
            pltpu.VMEM((NF, 8, 128), F32),
            pltpu.VMEM((NZ, NX, 8, 128), F32),
            pltpu.VMEM((NZ, NX, 8, 128), F32),
            dma((3,)),
            dma((ROUNDS,)), dma((ROUNDS,)),
            dma((ROUNDS,)), dma((ROUNDS,)),
            dma((ROUNDS, 2, 4)), dma((ROUNDS, 2, 4)),
            dma((ROUNDS, 2, 4)), dma((ROUNDS, 2, 4)),
            dma((ROUNDS, 3)), dma((ROUNDS, 3)),
            dma((ROUNDS, 4)), dma((ROUNDS, 4)),
            dma((ROUNDS, 2)), dma((ROUNDS, 2)),
            dma((10,)), dma((10,)),
            dma((7,)), dma((7,)),
            dma((7,)), dma((7,)),
            dma((10,)), dma((10,)),
        ],
        compiler_params=pltpu.CompilerParams(
            collective_id=0, has_side_effects=True, vmem_limit_bytes=60 * 2**20
        ),
    )(
        queries[0], keys[0], values[0], tokens_in[0], out_weight, pool, proj_weight, captions, valid_frames
    )
    return block_out[None], loss[0, 0:1]


def solution(mesh):
    placed = (
        P("dp", "frame", None),
        P("dp", "frame", None),
        P("dp", "frame", None),
        P("dp", "frame", None),
        P(None, "dp"),
        P(),
        P("frame", None),
        P("dp", None),
        P("dp"),
    )
    return jax.shard_map(
        local,
        mesh=mesh,
        in_specs=placed,
        out_specs=(P("dp", "frame", None), P("dp")),
        check_vma=False,
    )
```

time: 386 us -> 187 us (0.48)
  Pallas kernels: 0 us -> 177 us
  blocking collectives: 125 us -> 0 us
  matrix products: 85.8 us -> 0 us
  waiting for transfers between devices: 76.3 us -> 0 us
  local copies, waits for them, and re-layouts: 50.4 us -> 7.06 us
  between operations: 22 us -> 2.48 us
  starting transfers between devices: 17.8 us -> 0 us
  other arithmetic: 6.79 us -> 0 us
    pallas_call x0 -> x1, Pallas kernels: none -> 177 us  [local(): pl.pallas_call(body, out_shape=(jax.ShapeDtypeStruct((TOK, D), BF16), jax...]
    all_gather x3 -> x0, blocking collectives: 100 us -> none  [the longest x1 45 us: local(): lax.all_gather(sentence_embedding_matrix, 'dp', axis=0, tiled=True)]
    all_to_all x4 -> x0, waiting for transfers between devices: 75.6 us -> none  [the longest x1 23.9 us: local(): lax.all_to_all(attended, 'frame', split_axis=1, concat_axis=2, tiled=True)]
    dot_general x10 -> x0, matrix products: 45.7 us -> none  [the longest x4 29 us: one_block(): jnp.einsum('hqk,khd->qhd', weights, value_rows, preferred_element_type=jn...]
    sub x4 -> x0, matrix products: 40.1 us -> none  [one_block(): expo = jnp.exp(scores - peak)]
    unnamed x19 -> x5, local copies, waits for them, and re-layouts: 29.1 us -> 5.69 us
    all_to_all x4 -> x0, starting transfers between devices: 17.7 us -> none  [the longest x1 4.65 us: local(): lax.all_to_all(attended, 'frame', split_axis=1, concat_axis=2, tiled=True)]
    all_to_all x8 -> x0, local copies, waits for them, and re-layouts: 14.4 us -> none  [the longest x2 4.64 us: local(): lax.all_to_all(shaped_q, 'frame', split_axis=2, concat_axis=1, tiled=True)]
  transfers between devices with their start and end apart: 5 -> 0, of which waited for: 4 -> 0; matrix products, arithmetic and copies ran while one was open for 26% -> 0% of each run, Pallas kernels for 0% -> 0%
where the time goes in v1:
time: 187 us; the launch traced here: 186 us
  Pallas kernels  177 us (95%)
  local copies, waits for them, and re-layouts  7.06 us (4%)
  between operations  2.48 us (1%)
    pallas_call x1, Pallas kernels, local(): pl.pallas_call(body, out_shape=(jax.ShapeDtypeStruct((TOK, D), BF16), jax...  177 us
    unnamed x5, local copies, waits for them, and re-layouts  5.69 us

profile of v1, /device:TPU:4, one launch (start us, length us, event | category | flops | bytes accessed | tf_op | source)
XLA Modules:
  0.0 186.3 jit_solution(3279490629183620950)
XLA Ops:
  1.3 1.3 reshape.10
  2.7 0.7 copy.14
  3.4 2.3 %copy.11.w_hbm = bf16[3072,100]{1,0:T(8,128)(2,1)} copy(bf16[3072,100]{0,1:T(8,128)(2,1)} %param.13) | data formatting | bytes 1228800 | tf_op args[4]
  5.6 176.8 %shard_map.104 = (bf16[256,3200]{1,0:T(8,128)(2,1)}, f32[1,128]{1,0:T(1,128)}) custom-call(bf16[256,3072]{1,0:T(8,128)(2,1)} %bitcast.20, bf16[256,3072]{1,0:T(8,128)(2,1)} %bitcast.21, bf16[256,3072]{1,0:T(8,128)(2,1)} %bitcast.22, bf16[256,3200]{1,0:T(8,128)(2,1)} %bitcast.19, bf16[3072,100]{1,0:T(8,128)(2,1)} %copy.11.w_hbm, bf16[16,4096]{1,0:T(8,128)(2,1)} %bitcast.23, ...), custom_call_target="tpu_custom_call" | custom-call | tf_op jit(solution)/shard_map/pallas_call | solution.py:475
  182.4 0.0 copy-start
  182.4 2.7 %copy.18 = bf16[1,256,3200]{2,1,0:T(8,128)(2,1)} copy(bf16[1,256,3200]{2,1,0:T(8,128)(2,1)} %bitcast.18) | data formatting | bytes 3276800
  185.1 0.0 copy-done
  (1 shorter events, 0.0 us)
Async XLA Ops:
  182.4 2.7 %copy-start = (f32[1,128]{1,0:T(1,128)S(1)}, f32[1,128]{1,0:T(1,128)}, u32[]{:S(2)}) copy-start(f32[1,128]{1,0:T(1,128)} %get-tuple-element.5) | copy-start | bytes 1540

commit v2 on v1

v2 whole, which is shorter than its diff:
```python
import functools

import jax
import jax.numpy as jnp
from jax import lax
from jax.experimental import pallas as pl
from jax.experimental.pallas import tpu as pltpu
from jax.sharding import PartitionSpec as P

D = 3200
HEADS = 24
HD = 128
G = 16
TPF = 128
SEQ = 2048
TOK = 256
ROUNDS = 3
NF = 8
NZ = 8
NX = 4
KR = NF * HD
PIECE = 100
SCALE = 1.4426950408889634 / (128.0**0.5)
SHARP = 1.0 / 0.07

MESH = pl.DeviceIdType.MESH
F32 = jnp.float32
BF16 = jnp.bfloat16


def nt_dot(a, b):
    return lax.dot_general(a, b, (((1,), (1,)), ((), ())), preferred_element_type=F32)


def body(
    q_hbm, k_hbm, v_hbm, tok_hbm, w_hbm, pk_ref, proj_hbm, cap_ref, valid_ref,
    out_hbm, loss_ref,
    tok, wown, proj, own_a, own_x, stage_a, stage_x, m32, wt, qkv, k2, vext, osend, orecv, acc, blk,
    msg, pout, parts, emb, embs, caps, logit,
    lsem, qs, qr, os_, or_, as_, ar, x1s, x1r, z1s, z1r, z2s, z2r, x2s, x2r, x2f, sbs, sbr,
    cs, cr, ms, mr, es, er, gs, gr,
):
    dp = lax.axis_index("dp")
    f = lax.axis_index("frame")
    z = dp // NX
    x = lax.rem(dp, NX)
    c = lax.rem(f, 2)
    sib = f + 1 - 2 * c
    sign = 1 - 2 * c
    valid = valid_ref[0]
    right = lax.rem(x + 1, NX)
    left = lax.rem(x + NX - 1, NX)
    across = lax.rem(x + 2, NX)

    def at_z(zz):
        return {"dp": zz * NX + x}

    def at_x(xx):
        return {"dp": z * NX + xx}

    def remote(src, dst, ssem, rsem, where):
        return pltpu.make_async_remote_copy(
            src_ref=src, dst_ref=dst, send_sem=ssem, recv_sem=rsem, device_id=where, device_id_type=MESH
        )

    def sent(ref, sem):
        pltpu.make_async_copy(ref, ref, sem).wait()

    loads = [
        pltpu.make_async_copy(w_hbm, wown, lsem.at[0]),
        pltpu.make_async_copy(tok_hbm, tok, lsem.at[1]),
        pltpu.make_async_copy(proj_hbm, proj, lsem.at[2]),
    ]
    for load in loads:
        load.start()

    barrier = pltpu.get_barrier_semaphore()
    for i in range(1, NF):
        pl.semaphore_signal(barrier, inc=1, device_id={"frame": lax.rem(f + i, NF)}, device_id_type=MESH)
    for i in range(1, NX):
        pl.semaphore_signal(barrier, inc=1, device_id=at_x(lax.rem(x + i, NX)), device_id_type=MESH)
    for i in range(1, NZ):
        pl.semaphore_signal(barrier, inc=1, device_id=at_z(lax.rem(z + i, NZ)), device_id_type=MESH)

    half = pl.multiple_of(c * 512, 512)
    loads[0].wait()
    for to in range(NX):
        for tile in range(2):
            lanes = pl.ds(pl.multiple_of((tile + 1) * KR + half + to * 128, 128), 128)
            own_a[to, 0:PIECE, 128 * tile : 128 * (tile + 1)] = wown[:, lanes]
    own_x[0:PIECE, :] = wown[:, pl.ds(half, 512)]
    for to in range(NX):
        own_a[to, 96:112, :] = jnp.concatenate([own_a[to, 96:112, :][0:4], jnp.zeros((12, 256), BF16)], axis=0)
    own_x[96:112, :] = jnp.concatenate([own_x[96:112, :][0:4], jnp.zeros((12, 512), BF16)], axis=0)
    pl.semaphore_wait(barrier, NF - 1 + NX - 1 + NZ - 1)

    def a_copy(i, src):
        to = lax.rem(x + i, NX)
        return remote(own_a.at[to], stage_a.at[src], as_, ar.at[i - 1], at_x(to))

    def x1_copy(i, src):
        return remote(own_x, stage_x.at[src], x1s, x1r.at[i - 1], at_x(lax.rem(x + i, NX)))

    def owner_lanes(tile, xx):
        return pl.ds(pl.multiple_of((tile + 1) * KR + half + xx * 128, 128), 128)

    def half_lanes(h):
        return pl.ds(pl.multiple_of(half + 256 * h, 256), 256)

    def block_rows(zb):
        return pl.ds(pl.multiple_of(400 * zb, 16), 400)

    def zmove(way, step):
        s = sign if way == 0 else -sign
        return lax.rem(z - s * step + NZ, NZ)

    def znext(way):
        s = sign if way == 0 else -sign
        return lax.rem(z + s + NZ, NZ)

    LAST = (4, 3)

    def z2_copy(tile, way, step):
        ref = wt.at[block_rows(zmove(way, step)), owner_lanes(tile, x)]
        return remote(ref, ref, z2s, z2r.at[tile, way, step], at_z(znext(way)))

    def z2_in(tile, way, step):
        ref = wt.at[block_rows(zmove(way, step)), owner_lanes(tile, x)]
        return remote(ref, ref, z2s, z2r.at[tile, way, step - 1], at_z(znext(way)))

    def z1_copy(h, way, step):
        ref = wt.at[block_rows(zmove(way, step)), half_lanes(h)]
        return remote(ref, ref, z1s, z1r.at[h, way, step], at_z(znext(way)))

    def z1_in(h, way, step):
        ref = wt.at[block_rows(zmove(way, step)), half_lanes(h)]
        return remote(ref, ref, z1s, z1r.at[h, way, step - 1], at_z(znext(way)))

    def place(o):
        return zmove(0, (o + 1) // 2) if o % 2 else zmove(1, o // 2)

    def x2_copy(tile, way, o, xx):
        ref = wt.at[block_rows(place(o)), owner_lanes(tile, xx)]
        return remote(ref, ref, x2s, x2r.at[tile, way, o], at_x(right if way == 0 else left))

    def x2_forward_copy(tile, way, o, xx):
        ref = wt.at[block_rows(place(o)), owner_lanes(tile, xx)]
        return remote(ref, ref, x2s, x2f.at[tile, o], at_x(right if way == 0 else left))

    def x2_own(tile, o):
        x2_copy(tile, 0, o, x).start()
        x2_copy(tile, 1, o, x).start()

    def x2_forward(tile, o):
        way, xx = ((0, left), (1, right))[o % 2]
        x2_copy(tile, way, o, xx).wait_recv()
        x2_forward_copy(tile, way, o, xx).start()

    def x2_near(tile):
        for o in range(NZ):
            way, xx = ((1, right), (0, left))[o % 2]
            x2_copy(tile, way, o, xx).wait_recv()

    def x2_far(tile):
        for o in range(NZ):
            x2_forward_copy(tile, o % 2, o, across).wait_recv()

    def z2_start(tile):
        for way in range(2):
            z2_copy(tile, way, 0).start()
        x2_own(tile, 0)

    def z2_step(tile, step):
        for way in range(2):
            if step <= LAST[way]:
                z2_in(tile, way, step).wait_recv()
                if step < LAST[way]:
                    z2_copy(tile, way, step).start()
                x2_own(tile, 2 * step - 1 if way == 0 else 2 * step)

    def z1_start(h):
        for way in range(2):
            z1_copy(h, way, 0).start()

    def z1_step(h, step):
        for way in range(2):
            if step <= LAST[way]:
                z1_in(h, way, step).wait_recv()
                if step < LAST[way]:
                    z1_copy(h, way, step).start()

    def sib_copy(which, core):
        base = core * 512
        if which == 0:
            lanes = pl.ds(pl.multiple_of(base, 512), 512)
        elif which == 1:
            lanes = pl.ds(pl.multiple_of(KR + base, 512), 512)
        else:
            xx = (x, left, right, across)[which - 2]
            lanes = pl.ds(pl.multiple_of(2 * KR + base + xx * 128, 128), 128)
        ref = wt.at[:, lanes]
        return remote(ref, ref, sbs, sbr.at[which], {"frame": sib})

    def sib_start(which):
        sib_copy(which, c).start()

    def sib_wait(which):
        sib_copy(which, 1 - c).wait_recv()

    def merge_a():
        stage_a[x] = own_a[x]
        for i in range(1, NX):
            a_copy(i, lax.rem(x - i + NX, NX)).wait_recv()
        for i in range(NX):
            m32[PIECE * i : PIECE * i + 112, 0:256] = stage_a[i].astype(F32)
        for tile in range(2):
            wt[block_rows(z), owner_lanes(tile, x)] = m32[0:400, 128 * tile : 128 * (tile + 1)].astype(BF16)

    def merge_x():
        stage_x[x] = own_x[...]
        for i in range(1, NX):
            x1_copy(i, lax.rem(x - i + NX, NX)).wait_recv()
        for i in range(NX):
            m32[PIECE * i : PIECE * i + 112, :] = stage_x[i].astype(F32)
        wt[block_rows(z), pl.ds(half, 512)] = m32[0:400, :].astype(BF16)

    def qkv_start(r):
        for i in range(1, NF):
            t = lax.rem(f + i, NF)
            cols = pl.ds(pl.multiple_of((r * NF + t) * HD, HD), HD)
            for a, ref in enumerate((k_hbm, v_hbm, q_hbm)):
                remote(
                    ref.at[:, cols],
                    qkv.at[r, a, pl.ds(pl.multiple_of(f * TOK, TOK), TOK), :],
                    qs.at[r], qr.at[r], {"frame": t},
                ).start()
        cols = pl.ds(pl.multiple_of((r * NF + f) * HD, HD), HD)
        for a, ref in enumerate((k_hbm, v_hbm, q_hbm)):
            pltpu.make_async_copy(
                ref.at[:, cols], qkv.at[r, a, pl.ds(pl.multiple_of(f * TOK, TOK), TOK), :], qr.at[r]
            ).start()

    def qkv_wait(r):
        pltpu.make_async_copy(qkv.at[r], qkv.at[r], qr.at[r]).wait()

    def prepare(r):
        for i in range(8):
            rows = slice(256 * i, 256 * (i + 1))
            live = (lax.broadcasted_iota(jnp.int32, (256, HD), 0) + 256 * i) // TPF < valid
            kk = qkv[r, 0, rows, :].astype(F32)
            first = qkv[r, 0, 0:16, :].astype(F32)[0:1, :]
            kk = jnp.where(live, kk, jnp.broadcast_to(first, (256, HD))) * SCALE
            hi = kk.astype(BF16)
            k2[rows, 0:HD] = hi
            k2[rows, HD : 2 * HD] = (kk - hi.astype(F32)).astype(BF16)
            vext[rows, 0:HD] = jnp.where(live, qkv[r, 1, rows, :].astype(F32), 0.0).astype(BF16)
            vext[rows, HD : 2 * HD] = jnp.where(live, 1.0, 0.0).astype(BF16)

    def attend(r, group):
        heads = pl.ds(pl.multiple_of(r * KR + f * HD, HD), HD)
        for g in range(0, NF, group):
            for i in range(g, g + group):
                b = lax.rem(f + 1 + i, NF)
                qq = qkv[r, 2, pl.ds(pl.multiple_of(b * TOK, TOK), TOK), :]
                scores = nt_dot(jnp.concatenate([qq, qq], axis=1), k2[...])
                peak = jnp.max(scores, axis=1, keepdims=True)
                weights = jnp.exp2(scores - peak).astype(BF16)
                both = jnp.dot(weights, vext[...], preferred_element_type=F32)
                osend[r, b] = (both[:, 0:HD] / both[:, HD : 2 * HD]).astype(BF16)
            for i in range(g, g + group):
                b = lax.rem(f + 1 + i, NF)
                if i < NF - 1:
                    remote(osend.at[r, b], orecv.at[:, heads], os_.at[r], or_.at[r], {"frame": b}).start()
                else:
                    pltpu.make_async_copy(osend.at[r, b], orecv.at[:, heads], or_.at[r]).start()

    def attended_wait(r):
        cols = orecv.at[:, pl.ds(r * KR, KR)]
        pltpu.make_async_copy(cols, cols, or_.at[r]).wait()

    def project(r):
        def step(n, carry):
            cols = pl.ds(pl.multiple_of(n * 640, 128), 640)
            rows = pl.ds(pl.multiple_of(n * 640, 128), 640)
            part = nt_dot(orecv[:, r * KR : (r + 1) * KR], wt[rows, r * KR : (r + 1) * KR])
            if r == 0:
                acc[:, cols] = tok[:, cols].astype(F32) + part
            elif r < ROUNDS - 1:
                acc[:, cols] += part
            else:
                blk[:, cols] = (acc[:, cols] + part).astype(BF16)
            return carry

        lax.fori_loop(0, 5, step, 0)

    for i in range(1, NX):
        a_copy(i, x).start()
    for i in range(1, NX):
        x1_copy(i, x).start()
    qkv_start(0)
    merge_a()
    z2_start(0)
    z2_start(1)
    qkv_start(1)
    qkv_start(2)

    for n in range(8):
        emb[0, n : n + 1, :] = cap_ref[0:1, 128 * n : 128 * (n + 1)]
    own_cap = emb[0]
    norm = jnp.sqrt(jnp.sum(own_cap * own_cap, keepdims=True) + 1e-06)
    caps[z, x] = own_cap / norm

    def cap_x(i, xx):
        ref = caps.at[z, xx]
        return remote(ref, ref, cs.at[0], cr.at[i - 1], at_x(lax.rem(x + i, NX)))

    def cap_z(i, zz):
        ref = caps.at[zz]
        return remote(ref, ref, cs.at[1], cr.at[NX - 2 + i], at_z(lax.rem(z + i, NZ)))

    for i in range(1, NX):
        cap_x(i, x).start()

    z2_step(0, 1)
    z2_step(1, 1)
    merge_x()
    z1_start(0)
    z2_step(0, 2)
    z2_step(1, 2)
    z1_start(1)
    for i in range(1, NX):
        cap_x(i, lax.rem(x - i + NX, NX)).wait_recv()
    for i in range(1, NZ):
        cap_z(i, z).start()
    z2_step(0, 3)
    z2_step(1, 3)
    z2_step(0, 4)
    z2_step(1, 4)

    qkv_wait(0)
    prepare(0)
    attend(0, 8)

    z1_step(0, 1)
    z1_step(1, 1)
    x2_forward(0, 0)
    x2_forward(0, 1)
    x2_forward(0, 2)
    z1_step(0, 2)
    x2_forward(0, 3)
    x2_forward(0, 4)
    z1_step(1, 2)

    qkv_wait(1)
    prepare(1)
    attend(1, 8)

    sib_start(2)
    x2_forward(0, 5)
    x2_forward(0, 6)
    z1_step(0, 3)
    z1_step(1, 3)
    x2_forward(0, 7)
    for o in range(4):
        x2_forward(1, o)
    z1_step(0, 4)
    z1_step(1, 4)
    sib_start(0)

    qkv_wait(2)
    prepare(2)
    attend(2, 4)

    for o in range(4, 8):
        x2_forward(1, o)
    x2_near(0)
    x2_far(0)
    sib_start(1)
    x2_near(1)
    sib_start(3)
    sib_start(4)
    loads[1].wait()
    loads[2].wait()
    sib_wait(0)
    attended_wait(0)
    project(0)
    sib_wait(1)
    attended_wait(1)
    project(1)
    x2_far(1)
    sib_start(5)
    for i in range(1, NZ):
        cap_z(i, lax.rem(z - i + NZ, NZ)).wait_recv()
    for which in range(2, 6):
        sib_wait(which)
    attended_wait(2)
    project(2)
    store = pltpu.make_async_copy(blk, out_hbm, lsem.at[0])
    store.start()

    scores = nt_dot(pk_ref[...], blk[...])
    token = lax.broadcasted_iota(jnp.int32, (G, TOK), 1) + f * TOK
    live = token // TPF < valid
    masked = jnp.where(live, scores, -1e30)
    peak = jnp.max(masked, axis=1, keepdims=True)
    expo = jnp.where(live, jnp.exp(masked - peak), 0.0)
    total = jnp.sum(expo, axis=1, keepdims=True)
    e0 = expo.astype(BF16)
    rest = expo - e0.astype(F32)
    e1 = rest.astype(BF16)
    e2 = (rest - e1.astype(F32)).astype(BF16)
    w48 = jnp.dot(jnp.concatenate([e0, e1, e2], axis=0), blk[...], preferred_element_type=F32)
    w16 = w48[0:G] + w48[G : 2 * G] + w48[2 * G : 3 * G]
    mine = lax.broadcasted_iota(jnp.int32, (G, D), 1) // (D // G) == lax.broadcasted_iota(jnp.int32, (G, D), 0)

    def spread(value):
        return jnp.sum(jnp.where(mine, value, 0.0), axis=0, keepdims=True)

    msg[0:1, :] = spread(w16)
    msg[1:2, :] = spread(jnp.broadcast_to(peak, (G, D)))
    msg[2:3, :] = spread(jnp.broadcast_to(total, (G, D)))
    msg[3:8, :] = jnp.zeros((5, D), F32)
    for t in range(NF):
        pout[t, :, 400:512] = jnp.zeros((8, 112), F32)
        pout[t, :, 0:400] = msg[:, 400 * t : 400 * (t + 1)]

    def part_copy(i, src):
        t = lax.rem(f + i, NF)
        return remote(pout.at[t], parts.at[src], ms, mr.at[i - 1], {"frame": t})

    for i in range(1, NF):
        part_copy(i, f).start()
    parts[f] = pout[f]

    sent(stage_a.at[pl.ds(0, 3)], as_)
    sent(stage_x.at[pl.ds(0, 3)], x1s)
    sent(wt.at[pl.ds(0, 2800), pl.ds(0, 256)], z2s)
    sent(wt.at[pl.ds(0, 2800), pl.ds(0, 512)], z1s)
    sent(wt.at[:, pl.ds(0, 768)], x2s)
    sent(wt.at[:, pl.ds(0, 1536)], sbs)
    for r in range(ROUNDS):
        sent(qkv.at[r, :, pl.ds(0, SEQ - TOK), :], qs.at[r])
        sent(orecv.at[:, pl.ds(0, KR - HD)], os_.at[r])
    sent(caps.at[0, pl.ds(0, 3)], cs.at[0])
    sent(caps.at[pl.ds(0, 7)], cs.at[1])

    for i in range(1, NF):
        part_copy(i, lax.rem(f - i + NF, NF)).wait_recv()
    gathered = parts[...]
    peaks = gathered[:, 1, :]
    top = jnp.max(peaks, axis=0, keepdims=True)
    scale = jnp.exp(peaks - top)
    denominator = jnp.sum(gathered[:, 2, :] * scale, axis=0, keepdims=True)
    pooled = jnp.sum(gathered[:, 0, :] * scale, axis=0, keepdims=True) / denominator
    column = jnp.transpose(jnp.broadcast_to(pooled, (128, 512)))[0:400]
    for n in range(8):
        emb[0, n : n + 1, :] = jnp.sum(column * proj[:, 128 * n : 128 * (n + 1)], axis=0, keepdims=True)

    def emb_copy(i, src):
        return remote(emb.at[0], embs.at[src], es, er.at[i - 1], {"frame": lax.rem(f + i, NF)})

    for i in range(1, NF):
        emb_copy(i, f).start()
    embs[f] = emb[0]
    for i in range(1, NF):
        emb_copy(i, lax.rem(f - i + NF, NF)).wait_recv()
    raw = jnp.sum(embs[...], axis=0)
    clip = raw / jnp.sqrt(jnp.sum(raw * raw, keepdims=True) + 1e-06)

    products = jnp.sum(caps[...].reshape(NZ * NX, 8, 128) * clip[None], axis=1)
    square = jnp.concatenate([products, jnp.zeros((96, 128), F32)], axis=0)
    row = SHARP * jnp.sum(jnp.transpose(square), axis=0, keepdims=True)
    logit[z, x] = jnp.broadcast_to(row, (8, 128))

    def log_x(i, xx):
        ref = logit.at[z, xx]
        return remote(ref, ref, gs.at[0], gr.at[i - 1], at_x(lax.rem(x + i, NX)))

    def log_z(i, zz):
        ref = logit.at[zz]
        return remote(ref, ref, gs.at[1], gr.at[NX - 2 + i], at_z(lax.rem(z + i, NZ)))

    for i in range(1, NX):
        log_x(i, x).start()
    lane = lax.broadcasted_iota(jnp.int32, (1, 128), 1)
    own = jnp.where(lane < NZ * NX, row, -jnp.inf)
    own_top = jnp.max(own, axis=1, keepdims=True)
    row_lse = jnp.log(jnp.sum(jnp.exp(own - own_top), axis=1, keepdims=True)) + own_top
    for i in range(1, NX):
        log_x(i, lax.rem(x - i + NX, NX)).wait_recv()
    for i in range(1, NZ):
        log_z(i, z).start()
    sent(pout.at[pl.ds(0, 7)], ms)
    sent(embs.at[pl.ds(0, 7)], es)
    sent(logit.at[0, pl.ds(0, 3)], gs.at[0])
    store.wait()
    for i in range(1, NZ):
        log_z(i, lax.rem(z - i + NZ, NZ)).wait_recv()
    table = logit[...].reshape(NZ * NX, 8, 128)
    col_top = jnp.max(table, axis=0)
    col_lse = (jnp.log(jnp.sum(jnp.exp(table - col_top[None]), axis=0)) + col_top)[0:1, :]
    picked = jnp.where(lane == dp, 0.5 * col_lse - row, 0.0)
    value = 0.5 * row_lse + jnp.sum(picked, axis=1, keepdims=True)
    loss_ref[...] = jnp.broadcast_to(value, (1, 128))
    sent(logit.at[pl.ds(0, 7)], gs.at[1])


def local(
    queries, keys, values, tokens_in, out_weight, pool_keys, proj_weight, captions, valid_frames
):
    any_ = pl.BlockSpec(memory_space=pl.ANY)
    vmem = pl.BlockSpec(memory_space=pltpu.VMEM)
    smem = pl.BlockSpec(memory_space=pltpu.SMEM)
    dma = pltpu.SemaphoreType.DMA
    block_out, loss = pl.pallas_call(
        body,
        out_shape=(
            jax.ShapeDtypeStruct((TOK, D), BF16),
            jax.ShapeDtypeStruct((1, 128), F32),
        ),
        in_specs=[any_, any_, any_, any_, any_, vmem, any_, vmem, smem],
        out_specs=(any_, vmem),
        scratch_shapes=[
            pltpu.VMEM((TOK, D), BF16),
            pltpu.VMEM((PIECE, HEADS * HD), BF16),
            pltpu.VMEM((400, 1024), F32),
            pltpu.VMEM((NX, 112, 256), BF16),
            pltpu.VMEM((112, 512), BF16),
            pltpu.VMEM((NX, 112, 256), BF16),
            pltpu.VMEM((NX, 112, 512), BF16),
            pltpu.VMEM((416, 512), F32),
            pltpu.VMEM((D, HEADS * HD), BF16),
            pltpu.VMEM((ROUNDS, 3, SEQ, HD), BF16),
            pltpu.VMEM((SEQ, 2 * HD), BF16),
            pltpu.VMEM((SEQ, 2 * HD), BF16),
            pltpu.VMEM((ROUNDS, NF, TOK, HD), BF16),
            pltpu.VMEM((TOK, HEADS * HD), BF16),
            pltpu.VMEM((TOK, D), F32),
            pltpu.VMEM((TOK, D), BF16),
            pltpu.VMEM((8, D), F32),
            pltpu.VMEM((NF, 8, 512), F32),
            pltpu.VMEM((NF, 8, 512), F32),
            pltpu.VMEM((1, 8, 128), F32),
            pltpu.VMEM((NF, 8, 128), F32),
            pltpu.VMEM((NZ, NX, 8, 128), F32),
            pltpu.VMEM((NZ, NX, 8, 128), F32),
            dma((3,)),
            dma((ROUNDS,)), dma((ROUNDS,)),
            dma((ROUNDS,)), dma((ROUNDS,)),
            dma, dma((3,)),
            dma, dma((3,)),
            dma, dma((2, 2, 4)),
            dma, dma((2, 2, 4)),
            dma, dma((2, 2, NZ)), dma((2, NZ)),
            dma, dma((6,)),
            dma((2,)), dma((10,)),
            dma, dma((7,)),
            dma, dma((7,)),
            dma((2,)), dma((10,)),
        ],
        compiler_params=pltpu.CompilerParams(
            collective_id=0, has_side_effects=True, vmem_limit_bytes=60 * 2**20
        ),
    )(
        queries[0], keys[0], values[0], tokens_in[0], out_weight.T, pool_keys.T, proj_weight, captions, valid_frames
    )
    return block_out[None], loss[0, 0:1]


def solution(mesh):
    placed = (
        P("dp", "frame", None),
        P("dp", "frame", None),
        P("dp", "frame", None),
        P("dp", "frame", None),
        P(None, "dp"),
        P(),
        P("frame", None),
        P("dp", None),
        P("dp"),
    )
    return jax.shard_map(
        local,
        mesh=mesh,
        in_specs=placed,
        out_specs=(P("dp", "frame", None), P("dp")),
        check_vma=False,
    )
```

time: 187 us -> 121 us (0.65)
  Pallas kernels: 177 us -> 115 us
  local copies, waits for them, and re-layouts: 7.06 us -> 2.71 us
    pallas_call x1, Pallas kernels: 177 us -> 115 us  [local(): pl.pallas_call(body, out_shape=(jax.ShapeDtypeStruct((TOK, D), BF16), jax...]
    unnamed x5 -> x3, local copies, waits for them, and re-layouts: 5.69 us -> 2.71 us
where the time goes in v2:
time: 121 us; the launch traced here: 120 us
  Pallas kernels  115 us (95%)
  local copies, waits for them, and re-layouts  2.71 us (2%)
  between operations  2.46 us (2%)
    pallas_call x1, Pallas kernels, local(): pl.pallas_call(body, out_shape=(jax.ShapeDtypeStruct((TOK, D), BF16), jax...  115 us
    unnamed x3, local copies, waits for them, and re-layouts  2.71 us

profile of v2, /device:TPU:4, one launch (start us, length us, event | category | flops | bytes accessed | tf_op | source)
XLA Modules:
  0.0 119.9 jit_solution(2366389432599104253)
XLA Ops:
  1.3 114.8 %shard_map.104 = (bf16[256,3200]{1,0:T(8,128)(2,1)}, f32[1,128]{1,0:T(1,128)}) custom-call(bf16[256,3072]{1,0:T(8,128)(2,1)} %bitcast.11, bf16[256,3072]{1,0:T(8,128)(2,1)} %bitcast.12, bf16[256,3072]{1,0:T(8,128)(2,1)} %bitcast.13, bf16[256,3200]{1,0:T(8,128)(2,1)} %bitcast.9, bf16[100,3072]{1,0:T(8,128)(2,1)} %bitcast.14, bf16[16,3200]{1,0:T(8,128)(2,1)} %bitcast.15, ...), custom_call_target="tpu_custom_call" | custom-call | tf_op jit(solution)/shard_map/pallas_call | solution.py:515
  116.0 0.0 copy-start
  116.1 2.7 %copy.14 = bf16[1,256,3200]{2,1,0:T(8,128)(2,1)} copy(bf16[1,256,3200]{2,1,0:T(8,128)(2,1)} %bitcast.10) | data formatting | bytes 3276800
  118.8 0.0 copy-done
Async XLA Ops:
  116.0 2.7 %copy-start = (f32[1,128]{1,0:T(1,128)S(1)}, f32[1,128]{1,0:T(1,128)}, u32[]{:S(2)}) copy-start(f32[1,128]{1,0:T(1,128)} %get-tuple-element.5) | copy-start | bytes 1540

commit v3 on v2

v3 whole, which is shorter than its diff:
```python
import functools

import jax
import jax.numpy as jnp
from jax import lax
from jax.experimental import pallas as pl
from jax.experimental.pallas import tpu as pltpu
from jax.sharding import PartitionSpec as P

D = 3200
HEADS = 24
HD = 128
G = 16
TPF = 128
SEQ = 2048
TOK = 256
ROUNDS = 3
NF = 8
NZ = 8
NX = 4
KR = NF * HD
TILE_AT = (0, 2 * KR)
HALF_AT = KR
PIECE = 100
SCALE = 1.4426950408889634 / (128.0**0.5)
SHARP = 1.0 / 0.07
FAR_FIRST = (4, 3, 5, 2, 6, 1, 7)

MESH = pl.DeviceIdType.MESH
F32 = jnp.float32
BF16 = jnp.bfloat16


def nt_dot(a, b):
    return lax.dot_general(a, b, (((1,), (1,)), ((), ())), preferred_element_type=F32)


def body(
    q_hbm, k_hbm, v_hbm, tok_hbm, w_hbm, pk_hbm, proj_hbm, cap_hbm, valid_ref,
    blk, loss_ref,
    tok, wown, proj, pool, cap, own_a, own_x, stage_a, stage_x, m32, wt, qkv, k2, vext, osend, orecv, acc,
    msg, pout, parts, emb, embs, caps, logit,
    lsem, qs, qr, os_, or_, as_, ar, x1s, x1r, z1s, z1r, z2s, z2r, x2s, x2r, x2f, sbs, sbr,
    cs, cr, ms, mr, es, er, gs, gr,
):
    dp = lax.axis_index("dp")
    f = lax.axis_index("frame")
    z = dp // NX
    x = lax.rem(dp, NX)
    c = lax.rem(f, 2)
    sib = f + 1 - 2 * c
    sign = 1 - 2 * c
    valid = valid_ref[0]
    right = lax.rem(x + 1, NX)
    left = lax.rem(x + NX - 1, NX)
    across = lax.rem(x + 2, NX)

    def at_z(zz):
        return {"dp": zz * NX + x}

    def at_x(xx):
        return {"dp": z * NX + xx}

    def remote(src, dst, ssem, rsem, where):
        return pltpu.make_async_remote_copy(
            src_ref=src, dst_ref=dst, send_sem=ssem, recv_sem=rsem, device_id=where, device_id_type=MESH
        )

    def passed(ref, sem):
        pltpu.make_async_copy(ref, ref, sem).wait()

    loads = [
        pltpu.make_async_copy(w_hbm, wown, lsem.at[0]),
        pltpu.make_async_copy(tok_hbm, tok, lsem.at[1]),
        pltpu.make_async_copy(cap_hbm, cap, lsem.at[2]),
        pltpu.make_async_copy(proj_hbm, proj, lsem.at[3]),
        pltpu.make_async_copy(pk_hbm, pool, lsem.at[4]),
    ]
    for load in loads:
        load.start()

    barrier = pltpu.get_barrier_semaphore()
    for i in range(1, NF):
        pl.semaphore_signal(barrier, inc=1, device_id={"frame": lax.rem(f + i, NF)}, device_id_type=MESH)
    for i in range(1, NX):
        pl.semaphore_signal(barrier, inc=1, device_id=at_x(lax.rem(x + i, NX)), device_id_type=MESH)
    for i in range(1, NZ):
        pl.semaphore_signal(barrier, inc=1, device_id=at_z(lax.rem(z + i, NZ)), device_id_type=MESH)

    half = pl.multiple_of(c * 512, 512)
    pl.semaphore_wait(barrier, NF - 1 + NX - 1 + NZ - 1)

    def a_copy(i, src):
        to = lax.rem(x + i, NX)
        return remote(own_a.at[to], stage_a.at[src], as_, ar.at[i - 1], at_x(to))

    def x1_copy(i, src):
        return remote(own_x, stage_x.at[src], x1s, x1r.at[i - 1], at_x(lax.rem(x + i, NX)))

    def owner_lanes(tile, xx):
        return pl.ds(pl.multiple_of(TILE_AT[tile] + half + xx * 128, 128), 128)

    def half_lanes(h):
        return pl.ds(pl.multiple_of(HALF_AT + half + 256 * h, 256), 256)

    def block_rows(zb):
        return pl.ds(pl.multiple_of(400 * zb, 16), 400)

    def zmove(part, way, step):
        s = sign if way == part else -sign
        return lax.rem(z - s * step + NZ, NZ)

    def znext(part, way):
        s = sign if way == part else -sign
        return lax.rem(z + s + NZ, NZ)

    LAST = (4, 3)

    def z2_copy(tile, way, step, sem_step):
        ref = wt.at[block_rows(zmove(tile, way, step)), owner_lanes(tile, x)]
        return remote(ref, ref, z2s, z2r.at[tile, way, sem_step], at_z(znext(tile, way)))

    def z1_copy(h, way, step, sem_step):
        ref = wt.at[block_rows(zmove(h, way, step)), half_lanes(h)]
        return remote(ref, ref, z1s, z1r.at[h, way, sem_step], at_z(znext(h, way)))

    def place(tile, o):
        return zmove(tile, 0, (o + 1) // 2) if o % 2 else zmove(tile, 1, o // 2)

    def x2_copy(tile, way, o, xx):
        ref = wt.at[block_rows(place(tile, o)), owner_lanes(tile, xx)]
        return remote(ref, ref, x2s, x2r.at[tile, way, o], at_x(right if way == 0 else left))

    def x2_forward_copy(tile, way, o, xx):
        ref = wt.at[block_rows(place(tile, o)), owner_lanes(tile, xx)]
        return remote(ref, ref, x2s, x2f.at[tile, o], at_x(right if way == 0 else left))

    def x2_own(tile, o):
        x2_copy(tile, 0, o, x).start()
        x2_copy(tile, 1, o, x).start()

    def x2_forward(tile, o):
        way, xx = ((0, left), (1, right))[o % 2]
        x2_copy(tile, way, o, xx).wait_recv()
        x2_forward_copy(tile, way, o, xx).start()

    def x2_near(tile):
        for o in range(NZ):
            way, xx = ((1, right), (0, left))[o % 2]
            x2_copy(tile, way, o, xx).wait_recv()

    def x2_far(tile):
        for o in range(NZ):
            x2_forward_copy(tile, o % 2, o, across).wait_recv()

    def z2_start(tile):
        for way in range(2):
            z2_copy(tile, way, 0, 0).start()

    def z2_step(tile, step):
        for way in range(2):
            if step <= LAST[way]:
                z2_copy(tile, way, step, step - 1).wait_recv()
                if step < LAST[way]:
                    z2_copy(tile, way, step, step).start()
                x2_own(tile, 2 * step - 1 if way == 0 else 2 * step)

    def z1_start(h):
        for way in range(2):
            z1_copy(h, way, 0, 0).start()

    def z1_step(h, step):
        for way in range(2):
            if step <= LAST[way]:
                z1_copy(h, way, step, step - 1).wait_recv()
                if step < LAST[way]:
                    z1_copy(h, way, step, step).start()

    def sib_copy(which, core):
        base = core * 512
        if which == 0:
            lanes = pl.ds(pl.multiple_of(HALF_AT + base, 512), 512)
        else:
            tile, nth = divmod(which - 1, 4)
            xx = (x, left, right, across)[nth]
            lanes = pl.ds(pl.multiple_of(TILE_AT[tile] + base + xx * 128, 128), 128)
        ref = wt.at[:, lanes]
        return remote(ref, ref, sbs, sbr.at[which], {"frame": sib})

    def sib_start(which):
        sib_copy(which, c).start()

    def sib_wait(which):
        sib_copy(which, 1 - c).wait_recv()

    def merge_a():
        stage_a[x] = own_a[x]
        for i in range(1, NX):
            a_copy(i, lax.rem(x - i + NX, NX)).wait_recv()
        for i in range(NX):
            m32[PIECE * i : PIECE * i + 112, 0:256] = stage_a[i].astype(F32)
        for tile in range(2):
            wt[block_rows(z), owner_lanes(tile, x)] = m32[0:400, 128 * tile : 128 * (tile + 1)].astype(BF16)

    def merge_x():
        stage_x[x] = own_x[...]
        for i in range(1, NX):
            x1_copy(i, lax.rem(x - i + NX, NX)).wait_recv()
        for i in range(NX):
            m32[PIECE * i : PIECE * i + 112, :] = stage_x[i].astype(F32)
        wt[block_rows(z), pl.ds(pl.multiple_of(HALF_AT + half, 512), 512)] = m32[0:400, :].astype(BF16)

    def qkv_start(r):
        for i in range(1, NF):
            t = lax.rem(f + i, NF)
            cols = pl.ds(pl.multiple_of((r * NF + t) * HD, HD), HD)
            for a, ref in enumerate((k_hbm, v_hbm, q_hbm)):
                remote(
                    ref.at[:, cols],
                    qkv.at[r, a, pl.ds(pl.multiple_of(f * TOK, TOK), TOK), :],
                    qs.at[r], qr.at[r], {"frame": t},
                ).start()
        cols = pl.ds(pl.multiple_of((r * NF + f) * HD, HD), HD)
        for a, ref in enumerate((k_hbm, v_hbm, q_hbm)):
            pltpu.make_async_copy(
                ref.at[:, cols], qkv.at[r, a, pl.ds(pl.multiple_of(f * TOK, TOK), TOK), :], qr.at[r]
            ).start()

    def qkv_wait(r):
        pltpu.make_async_copy(qkv.at[r], qkv.at[r], qr.at[r]).wait()

    def prepare(r):
        for i in range(8):
            rows = slice(256 * i, 256 * (i + 1))
            live = (lax.broadcasted_iota(jnp.int32, (256, HD), 0) + 256 * i) // TPF < valid
            kk = qkv[r, 0, rows, :].astype(F32)
            first = qkv[r, 0, 0:16, :].astype(F32)[0:1, :]
            kk = jnp.where(live, kk, jnp.broadcast_to(first, (256, HD))) * SCALE
            hi = kk.astype(BF16)
            k2[rows, 0:HD] = hi
            k2[rows, HD : 2 * HD] = (kk - hi.astype(F32)).astype(BF16)
            vext[rows, 0:HD] = jnp.where(live, qkv[r, 1, rows, :].astype(F32), 0.0).astype(BF16)
            vext[rows, HD : 2 * HD] = jnp.where(live, 1.0, 0.0).astype(BF16)

    def attend(r, start, stop):
        for i in range(start, stop):
            b = lax.rem(f + 1 + i, NF)
            qq = qkv[r, 2, pl.ds(pl.multiple_of(b * TOK, TOK), TOK), :]
            scores = nt_dot(jnp.concatenate([qq, qq], axis=1), k2[...])
            peak = jnp.max(scores, axis=1, keepdims=True)
            weights = jnp.exp2(scores - peak).astype(BF16)
            both = jnp.dot(weights, vext[...], preferred_element_type=F32)
            osend[r, b] = (both[:, 0:HD] / both[:, HD : 2 * HD]).astype(BF16)

    def give_back(r, start, stop):
        group = r + start // 4
        heads = pl.ds(pl.multiple_of(r * KR + f * HD, HD), HD)
        for i in range(start, stop):
            b = lax.rem(f + 1 + i, NF)
            if i < NF - 1:
                remote(osend.at[r, b], orecv.at[:, heads], os_.at[r], or_.at[group], {"frame": b}).start()
            else:
                pltpu.make_async_copy(osend.at[r, b], orecv.at[:, heads], or_.at[group]).start()

    def attended_wait(r):
        cols = orecv.at[:, pl.ds(r * KR, KR)]
        pltpu.make_async_copy(cols, cols, or_.at[r]).wait()

    def blocks_of_columns(step):
        def one(n, carry):
            return step(pl.ds(pl.multiple_of(n * 1024, 128), 1024), carry)

        return step(pl.ds(3072, 128), lax.fori_loop(0, 3, one, jnp.zeros((G, TOK), F32)))

    def project(r):
        def step(cols, carry):
            part = nt_dot(orecv[:, r * KR : (r + 1) * KR], wt[cols, r * KR : (r + 1) * KR])
            if r == 0:
                acc[:, cols] = tok[:, cols].astype(F32) + part
            else:
                acc[:, cols] += part
            return carry

        blocks_of_columns(step)

    def project_last(group):
        cols = orecv.at[:, pl.ds(0, 4 * HD)]
        pltpu.make_async_copy(cols, cols, or_.at[2 + group]).wait()
        lanes = []
        for i in range(1, 5):
            source = lax.rem(f - i - 4 * group + 2 * NF, NF)
            lanes.append(pl.ds(pl.multiple_of(2 * KR + source * HD, HD), HD))
        rows = jnp.concatenate([orecv[:, ln] for ln in lanes], axis=1)

        def step(cols, carry):
            part = nt_dot(rows, jnp.concatenate([wt[cols, ln] for ln in lanes], axis=1))
            if group == 0:
                acc[:, cols] += part
                return carry
            block = (acc[:, cols] + part).astype(BF16)
            blk[:, cols] = block
            return carry + nt_dot(pool[:, cols], block)

        return blocks_of_columns(step)

    qkv_start(0)

    loads[0].wait()
    for to in range(NX):
        for tile in range(2):
            lanes = pl.ds(pl.multiple_of(TILE_AT[tile] + half + to * 128, 128), 128)
            own_a[to, 0:PIECE, 128 * tile : 128 * (tile + 1)] = wown[:, lanes]
    own_x[0:PIECE, :] = wown[:, pl.ds(pl.multiple_of(HALF_AT + half, 512), 512)]
    for to in range(NX):
        own_a[to, 96:112, :] = jnp.concatenate([own_a[to, 96:112, :][0:4], jnp.zeros((12, 256), BF16)], axis=0)
    own_x[96:112, :] = jnp.concatenate([own_x[96:112, :][0:4], jnp.zeros((12, 512), BF16)], axis=0)
    for i in range(1, NX):
        a_copy(i, x).start()
    merge_a()
    z2_start(0)
    z2_start(1)
    for i in range(1, NX):
        x1_copy(i, x).start()
    x2_own(0, 0)
    x2_own(1, 0)
    qkv_start(1)
    qkv_start(2)

    loads[2].wait()
    for n in range(8):
        emb[0, n : n + 1, :] = cap[0:1, 128 * n : 128 * (n + 1)]
    own_cap = emb[0]
    norm = jnp.sqrt(jnp.sum(own_cap * own_cap, keepdims=True) + 1e-06)
    caps[z, x] = own_cap / norm

    def cap_x(i, xx):
        ref = caps.at[z, xx]
        return remote(ref, ref, cs.at[0], cr.at[i - 1], at_x(lax.rem(x + i, NX)))

    def cap_z(i, zz):
        ref = caps.at[zz]
        return remote(ref, ref, cs.at[1], cr.at[NX - 2 + i], at_z(lax.rem(z + i, NZ)))

    for i in range(1, NX):
        cap_x(i, x).start()

    z2_step(0, 1)
    z2_step(1, 1)
    z2_step(0, 2)
    z2_step(1, 2)
    merge_x()
    z1_start(0)
    z2_step(0, 3)
    z2_step(1, 3)
    z1_start(1)
    for i in range(1, NX):
        cap_x(i, lax.rem(x - i + NX, NX)).wait_recv()
    for i in range(1, NZ):
        cap_z(i, z).start()

    qkv_wait(0)
    prepare(0)
    attend(0, 0, 2)
    z2_step(0, 4)
    z2_step(1, 4)
    z1_step(0, 1)
    attend(0, 2, 6)
    z1_step(1, 1)
    attend(0, 6, 8)
    for o in range(0, 3):
        x2_forward(0, o)
    z1_step(0, 2)
    for o in range(3, 6):
        x2_forward(0, o)

    qkv_wait(1)
    prepare(1)
    attend(1, 0, 2)
    z1_step(1, 2)
    sib_start(1)
    sib_start(5)
    attend(1, 2, 5)
    z1_step(0, 3)
    x2_forward(0, 6)
    x2_forward(0, 7)
    x2_near(0)
    sib_start(2)
    sib_start(3)
    for o in range(0, 4):
        x2_forward(1, o)
    give_back(0, 0, 8)
    attend(1, 5, 8)
    give_back(1, 0, 8)
    z1_step(1, 3)
    for o in range(4, 8):
        x2_forward(1, o)
    x2_near(1)
    sib_start(6)
    sib_start(7)

    qkv_wait(2)
    prepare(2)
    attend(2, 0, 4)
    give_back(2, 0, 4)
    x2_far(0)
    sib_start(4)
    z1_step(0, 4)
    z1_step(1, 4)
    sib_start(0)
    attend(2, 4, 8)
    give_back(2, 4, 8)

    loads[1].wait()
    loads[3].wait()
    loads[4].wait()
    for which in range(1, 5):
        sib_wait(which)
    attended_wait(0)
    project(0)
    x2_far(1)
    sib_start(8)
    sib_wait(0)
    attended_wait(1)
    project(1)
    for i in range(1, NZ):
        cap_z(i, lax.rem(z - i + NZ, NZ)).wait_recv()
    for which in range(5, 9):
        sib_wait(which)
    project_last(0)
    scores = project_last(1)

    token = lax.broadcasted_iota(jnp.int32, (G, TOK), 1) + f * TOK
    live = token // TPF < valid
    masked = jnp.where(live, scores, -1e30)
    peak = jnp.max(masked, axis=1, keepdims=True)
    expo = jnp.where(live, jnp.exp(masked - peak), 0.0)
    total = jnp.sum(expo, axis=1, keepdims=True)
    e0 = expo.astype(BF16)
    rest = expo - e0.astype(F32)
    e1 = rest.astype(BF16)
    e2 = (rest - e1.astype(F32)).astype(BF16)
    w48 = jnp.dot(jnp.concatenate([e0, e1, e2], axis=0), blk[...], preferred_element_type=F32)
    w16 = w48[0:G] + w48[G : 2 * G] + w48[2 * G : 3 * G]
    mine = lax.broadcasted_iota(jnp.int32, (G, D), 1) // (D // G) == lax.broadcasted_iota(jnp.int32, (G, D), 0)

    msg[...] = jnp.sum(jnp.where(mine, w16, 0.0), axis=0, keepdims=True)
    stats = jnp.concatenate([peak, total], axis=1)
    for t in range(NF):
        pout[t, :, 0:400] = msg[:, 400 * t : 400 * (t + 1)]
        pout[t, :, 400:402] = stats[2 * t : 2 * t + 1, :]
        pout[t, :, 402:404] = stats[2 * t + 1 : 2 * t + 2, :]

    def part_copy(i, src):
        t = lax.rem(f + i, NF)
        return remote(pout.at[t], parts.at[src], ms, mr, {"frame": t})

    for i in FAR_FIRST:
        part_copy(i, f).start()
    parts[f] = pout[f]

    passed(stage_a.at[pl.ds(0, 3)], as_)
    passed(stage_x.at[pl.ds(0, 3)], x1s)
    passed(wt.at[pl.ds(0, 2800), pl.ds(0, 256)], z2s)
    passed(wt.at[pl.ds(0, 2800), pl.ds(0, 512)], z1s)
    passed(wt.at[:, pl.ds(0, 768)], x2s)
    passed(wt.at[:, pl.ds(0, 1536)], sbs)
    for r in range(ROUNDS):
        passed(qkv.at[r, :, pl.ds(0, SEQ - TOK), :], qs.at[r])
        passed(orecv.at[:, pl.ds(0, KR - HD)], os_.at[r])
    passed(caps.at[0, pl.ds(0, 3)], cs.at[0])
    passed(caps.at[pl.ds(0, 7)], cs.at[1])

    passed(parts.at[pl.ds(0, NF - 1)], mr)
    gathered = parts[...].reshape(NF, 512)
    first = lax.broadcasted_iota(jnp.int32, (NF, 512), 1) < D // G
    peaks = jnp.where(first, gathered[:, 400:401], gathered[:, 402:403])
    totals = jnp.where(first, gathered[:, 401:402], gathered[:, 403:404])
    top = jnp.max(peaks, axis=0, keepdims=True)
    scale = jnp.exp(peaks - top)
    denominator = jnp.sum(totals * scale, axis=0, keepdims=True)
    pooled = jnp.sum(gathered * scale, axis=0, keepdims=True) / denominator
    column = jnp.transpose(jnp.broadcast_to(pooled, (128, 512)))[0:400]
    for n in range(8):
        emb[0, n : n + 1, :] = jnp.sum(column * proj[:, 128 * n : 128 * (n + 1)], axis=0, keepdims=True)

    def emb_copy(i, src):
        return remote(emb.at[0], embs.at[src], es, er, {"frame": lax.rem(f + i, NF)})

    for i in FAR_FIRST:
        emb_copy(i, f).start()
    embs[f] = emb[0]
    passed(embs.at[pl.ds(0, NF - 1)], er)
    raw = jnp.sum(embs[...], axis=0)
    clip = raw / jnp.sqrt(jnp.sum(raw * raw, keepdims=True) + 1e-06)

    products = jnp.sum(caps[...].reshape(NZ * NX, 8, 128) * clip[None], axis=1)
    square = jnp.concatenate([products, jnp.zeros((96, 128), F32)], axis=0)
    row = SHARP * jnp.sum(jnp.transpose(square), axis=0, keepdims=True)
    logit[dp] = row

    def log_copy(i, src):
        ref = logit.at[src]
        to = lax.rem(dp + i, NZ * NX)
        return remote(ref, ref, gs, gr, {"dp": to})

    def log_start(i, carry):
        log_copy(1 + lax.rem(i + 11, NZ * NX - 1), dp).start()
        return carry

    lax.fori_loop(0, NZ * NX - 1, log_start, 0)
    lane = lax.broadcasted_iota(jnp.int32, (1, 128), 1)
    own = jnp.where(lane < NZ * NX, row, -jnp.inf)
    own_top = jnp.max(own, axis=1, keepdims=True)
    row_lse = jnp.log(jnp.sum(jnp.exp(own - own_top), axis=1, keepdims=True)) + own_top
    passed(pout.at[pl.ds(0, 7)], ms)
    passed(embs.at[pl.ds(0, 7)], es)

    passed(logit.at[pl.ds(0, NZ * NX - 1)], gr)
    table = logit[...].reshape(NZ * NX, 128)
    col_top = jnp.max(table, axis=0, keepdims=True)
    col_lse = jnp.log(jnp.sum(jnp.exp(table - col_top), axis=0, keepdims=True)) + col_top
    picked = jnp.where(lane == dp, 0.5 * col_lse - row, 0.0)
    value = 0.5 * row_lse + jnp.sum(picked, axis=1, keepdims=True)
    loss_ref[...] = jnp.broadcast_to(value, (1, 128))
    passed(logit.at[pl.ds(0, NZ * NX - 1)], gs)


def local(
    queries, keys, values, tokens_in, out_weight, pool_keys, proj_weight, captions, valid_frames
):
    any_ = pl.BlockSpec(memory_space=pl.ANY)
    vmem = pl.BlockSpec(memory_space=pltpu.VMEM)
    smem = pl.BlockSpec(memory_space=pltpu.SMEM)
    dma = pltpu.SemaphoreType.DMA
    block_out, loss = pl.pallas_call(
        body,
        out_shape=(
            pltpu.VMEM((TOK, D), BF16),
            jax.ShapeDtypeStruct((1, 128), F32),
        ),
        in_specs=[any_, any_, any_, any_, any_, any_, any_, any_, smem],
        out_specs=(vmem, vmem),
        scratch_shapes=[
            pltpu.VMEM((TOK, D), BF16),
            pltpu.VMEM((PIECE, HEADS * HD), BF16),
            pltpu.VMEM((400, 1024), F32),
            pltpu.VMEM((G, D), BF16),
            pltpu.VMEM((1, 1024), F32),
            pltpu.VMEM((NX, 112, 256), BF16),
            pltpu.VMEM((112, 512), BF16),
            pltpu.VMEM((NX, 112, 256), BF16),
            pltpu.VMEM((NX, 112, 512), BF16),
            pltpu.VMEM((416, 512), F32),
            pltpu.VMEM((D, HEADS * HD), BF16),
            pltpu.VMEM((ROUNDS, 3, SEQ, HD), BF16),
            pltpu.VMEM((SEQ, 2 * HD), BF16),
            pltpu.VMEM((SEQ, 2 * HD), BF16),
            pltpu.VMEM((ROUNDS, NF, TOK, HD), BF16),
            pltpu.VMEM((TOK, HEADS * HD), BF16),
            pltpu.VMEM((TOK, D), F32),
            pltpu.VMEM((1, D), F32),
            pltpu.VMEM((NF, 1, 512), F32),
            pltpu.VMEM((NF, 1, 512), F32),
            pltpu.VMEM((1, 8, 128), F32),
            pltpu.VMEM((NF, 8, 128), F32),
            pltpu.VMEM((NZ, NX, 8, 128), F32),
            pltpu.VMEM((NZ * NX, 1, 128), F32),
            dma((5,)),
            dma((ROUNDS,)), dma((ROUNDS,)),
            dma((ROUNDS,)), dma((ROUNDS + 1,)),
            dma, dma((3,)),
            dma, dma((3,)),
            dma, dma((2, 2, 4)),
            dma, dma((2, 2, 4)),
            dma, dma((2, 2, NZ)), dma((2, NZ)),
            dma, dma((9,)),
            dma((2,)), dma((10,)),
            dma, dma,
            dma, dma,
            dma, dma,
        ],
        compiler_params=pltpu.CompilerParams(
            collective_id=0, has_side_effects=True, vmem_limit_bytes=60 * 2**20
        ),
    )(
        queries[0], keys[0], values[0], tokens_in[0], out_weight.T, pool_keys.T, proj_weight, captions, valid_frames
    )
    return block_out[None], loss[0, 0:1]


def solution(mesh):
    placed = (
        P("dp", "frame", None),
        P("dp", "frame", None),
        P("dp", "frame", None),
        P("dp", "frame", None),
        P(None, "dp"),
        P(),
        P("frame", None),
        P("dp", None),
        P("dp"),
    )
    return jax.shard_map(
        local,
        mesh=mesh,
        in_specs=placed,
        out_specs=(P("dp", "frame", None), P("dp")),
        check_vma=False,
    )
```

time: 121 us -> 102 us (0.84)
  Pallas kernels: 115 us -> 96.7 us
  local copies, waits for them, and re-layouts: 2.71 us -> 1.17 us
    pallas_call x1, Pallas kernels: 115 us -> 96.7 us  [local(): pl.pallas_call(body, out_shape=(pltpu.VMEM((TOK, D), BF16), jax.ShapeDtyp...]
    unnamed x3, local copies, waits for them, and re-layouts: 2.71 us -> 1.17 us
where the time goes in v3:
time: 102 us; the launch traced here: 100 us
  Pallas kernels  96.7 us (95%)
  between operations  2.46 us (2%)
  local copies, waits for them, and re-layouts  1.17 us (1%)
    pallas_call x1, Pallas kernels, local(): pl.pallas_call(body, out_shape=(pltpu.VMEM((TOK, D), BF16), jax.ShapeDtyp...  96.7 us

profile of v3, /device:TPU:4, one launch (start us, length us, event | category | flops | bytes accessed | tf_op | source)
XLA Modules:
  0.0 100.3 jit_solution(209947759249647744)
XLA Ops:
  1.3 96.7 %shard_map.104 = (bf16[256,3200]{1,0:T(8,128)(2,1)S(1)}, f32[1,128]{1,0:T(1,128)}) custom-call(bf16[256,3072]{1,0:T(8,128)(2,1)} %bitcast.11, bf16[256,3072]{1,0:T(8,128)(2,1)} %bitcast.12, bf16[256,3072]{1,0:T(8,128)(2,1)} %bitcast.13, bf16[256,3200]{1,0:T(8,128)(2,1)} %bitcast.10, bf16[100,3072]{1,0:T(8,128)(2,1)} %bitcast.14, bf16[16,3200]{1,0:T(8,128)(2,1)} %bitcast.15, ...), custom_call_target="tpu_custom_call" | custom-call | tf_op jit(solution)/shard_map/pallas_call | solution.py:535
  98.0 0.0 copy-start
  98.0 1.2 %copy.13 = bf16[1,256,3200]{2,1,0:T(8,128)(2,1)} copy(bf16[1,256,3200]{2,1,0:T(8,128)(2,1)S(1)} %bitcast.9) | data formatting | bytes 3276800
  99.2 0.0 copy-done
Async XLA Ops:
  98.0 1.2 %copy-start = (f32[1,128]{1,0:T(1,128)S(1)}, f32[1,128]{1,0:T(1,128)}, u32[]{:S(2)}) copy-start(f32[1,128]{1,0:T(1,128)} %get-tuple-element.5) | copy-start | bytes 1540

commit v4 on v3

--- a/solution.py
+++ b/solution.py
@@ -36,9 +36,9 @@
 
 
 def body(
-    q_hbm, k_hbm, v_hbm, tok_hbm, w_hbm, pk_hbm, proj_hbm, cap_hbm, valid_ref,
-    blk, loss_ref,
-    tok, wown, proj, pool, cap, own_a, own_x, stage_a, stage_x, m32, wt, qkv, k2, vext, osend, orecv, acc,
+    q_hbm, k_hbm, v_hbm, tok_hbm, w_hbm, pk_hbm, proj_hbm, cap_hbm, valid_hbm,
+    out_ref, loss_out,
+    tok, wown, proj, pool, cap, count, blk, loss, own_a, own_x, stage_a, stage_x, m32, wt, qkv, k2, vext, osend, orecv, acc,
     msg, pout, parts, emb, embs, caps, logit,
     lsem, qs, qr, os_, or_, as_, ar, x1s, x1r, z1s, z1r, z2s, z2r, x2s, x2r, x2f, sbs, sbr,
     cs, cr, ms, mr, es, er, gs, gr,
@@ -50,7 +50,6 @@
     c = lax.rem(f, 2)
     sib = f + 1 - 2 * c
     sign = 1 - 2 * c
-    valid = valid_ref[0]
     right = lax.rem(x + 1, NX)
     left = lax.rem(x + NX - 1, NX)
     across = lax.rem(x + 2, NX)
@@ -75,6 +74,7 @@
         pltpu.make_async_copy(cap_hbm, cap, lsem.at[2]),
         pltpu.make_async_copy(proj_hbm, proj, lsem.at[3]),
         pltpu.make_async_copy(pk_hbm, pool, lsem.at[4]),
+        pltpu.make_async_copy(valid_hbm, count, lsem.at[5]),
     ]
     for load in loads:
         load.start()
@@ -229,7 +229,7 @@
     def qkv_wait(r):
         pltpu.make_async_copy(qkv.at[r], qkv.at[r], qr.at[r]).wait()
 
-    def prepare(r):
+    def prepare(r, valid):
         for i in range(8):
             rows = slice(256 * i, 256 * (i + 1))
             live = (lax.broadcasted_iota(jnp.int32, (256, HD), 0) + 256 * i) // TPF < valid
@@ -266,11 +266,11 @@
         cols = orecv.at[:, pl.ds(r * KR, KR)]
         pltpu.make_async_copy(cols, cols, or_.at[r]).wait()
 
-    def blocks_of_columns(step):
+    def blocks_of_columns(step, unroll):
         def one(n, carry):
             return step(pl.ds(pl.multiple_of(n * 1024, 128), 1024), carry)
 
-        return step(pl.ds(3072, 128), lax.fori_loop(0, 3, one, jnp.zeros((G, TOK), F32)))
+        return step(pl.ds(3072, 128), lax.fori_loop(0, 3, one, jnp.zeros((G, TOK), F32), unroll=unroll))
 
     def project(r):
         def step(cols, carry):
@@ -281,7 +281,7 @@
                 acc[:, cols] += part
             return carry
 
-        blocks_of_columns(step)
+        blocks_of_columns(step, False)
 
     def project_last(group):
         cols = orecv.at[:, pl.ds(0, 4 * HD)]
@@ -301,7 +301,7 @@
             blk[:, cols] = block
             return carry + nt_dot(pool[:, cols], block)
 
-        return blocks_of_columns(step)
+        return blocks_of_columns(step, True)
 
     qkv_start(0)
 
@@ -327,6 +327,8 @@
     qkv_start(2)
 
     loads[2].wait()
+    loads[5].wait()
+    valid = count[...]
     for n in range(8):
         emb[0, n : n + 1, :] = cap[0:1, 128 * n : 128 * (n + 1)]
     own_cap = emb[0]
@@ -359,7 +361,7 @@
         cap_z(i, z).start()
 
     qkv_wait(0)
-    prepare(0)
+    prepare(0, valid)
     attend(0, 0, 2)
     z2_step(0, 4)
     z2_step(1, 4)
@@ -374,7 +376,7 @@
         x2_forward(0, o)
 
     qkv_wait(1)
-    prepare(1)
+    prepare(1, valid)
     attend(1, 0, 2)
     z1_step(1, 2)
     sib_start(1)
@@ -399,7 +401,7 @@
     sib_start(7)
 
     qkv_wait(2)
-    prepare(2)
+    prepare(2, valid)
     attend(2, 0, 4)
     give_back(2, 0, 4)
     x2_far(0)
@@ -456,6 +458,8 @@
 
     for i in FAR_FIRST:
         part_copy(i, f).start()
+    store = pltpu.make_async_copy(blk, out_ref, lsem.at[6])
+    store.start()
     parts[f] = pout[f]
 
     passed(stage_a.at[pl.ds(0, 3)], as_)
@@ -503,11 +507,8 @@
         to = lax.rem(dp + i, NZ * NX)
         return remote(ref, ref, gs, gr, {"dp": to})
 
-    def log_start(i, carry):
-        log_copy(1 + lax.rem(i + 11, NZ * NX - 1), dp).start()
-        return carry
-
-    lax.fori_loop(0, NZ * NX - 1, log_start, 0)
+    for i in range(NZ * NX - 1):
+        log_copy(1 + (i + 11) % (NZ * NX - 1), dp).start()
     lane = lax.broadcasted_iota(jnp.int32, (1, 128), 1)
     own = jnp.where(lane < NZ * NX, row, -jnp.inf)
     own_top = jnp.max(own, axis=1, keepdims=True)
@@ -515,37 +516,41 @@
     passed(pout.at[pl.ds(0, 7)], ms)
     passed(embs.at[pl.ds(0, 7)], es)
 
+    store.wait()
     passed(logit.at[pl.ds(0, NZ * NX - 1)], gr)
     table = logit[...].reshape(NZ * NX, 128)
     col_top = jnp.max(table, axis=0, keepdims=True)
     col_lse = jnp.log(jnp.sum(jnp.exp(table - col_top), axis=0, keepdims=True)) + col_top
     picked = jnp.where(lane == dp, 0.5 * col_lse - row, 0.0)
     value = 0.5 * row_lse + jnp.sum(picked, axis=1, keepdims=True)
-    loss_ref[...] = jnp.broadcast_to(value, (1, 128))
+    loss[...] = jnp.broadcast_to(value, (1, 128))
+    pltpu.make_async_copy(loss, loss_out, lsem.at[7]).start()
     passed(logit.at[pl.ds(0, NZ * NX - 1)], gs)
+    pltpu.make_async_copy(loss, loss_out, lsem.at[7]).wait()
 
 
 def local(
     queries, keys, values, tokens_in, out_weight, pool_keys, proj_weight, captions, valid_frames
 ):
     any_ = pl.BlockSpec(memory_space=pl.ANY)
-    vmem = pl.BlockSpec(memory_space=pltpu.VMEM)
-    smem = pl.BlockSpec(memory_space=pltpu.SMEM)
     dma = pltpu.SemaphoreType.DMA
     block_out, loss = pl.pallas_call(
         body,
         out_shape=(
             pltpu.VMEM((TOK, D), BF16),
-            jax.ShapeDtypeStruct((1, 128), F32),
+            pltpu.VMEM((1, 128), F32),
         ),
-        in_specs=[any_, any_, any_, any_, any_, any_, any_, any_, smem],
-        out_specs=(vmem, vmem),
+        in_specs=[any_, any_, any_, any_, any_, any_, any_, any_, any_],
+        out_specs=(any_, any_),
         scratch_shapes=[
             pltpu.VMEM((TOK, D), BF16),
             pltpu.VMEM((PIECE, HEADS * HD), BF16),
             pltpu.VMEM((400, 1024), F32),
             pltpu.VMEM((G, D), BF16),
             pltpu.VMEM((1, 1024), F32),
+            pltpu.VMEM((1, 1), jnp.int32),
+            pltpu.VMEM((TOK, D), BF16),
+            pltpu.VMEM((1, 128), F32),
             pltpu.VMEM((NX, 112, 256), BF16),
             pltpu.VMEM((112, 512), BF16),
             pltpu.VMEM((NX, 112, 256), BF16),
@@ -565,7 +570,7 @@
             pltpu.VMEM((NF, 8, 128), F32),
             pltpu.VMEM((NZ, NX, 8, 128), F32),
             pltpu.VMEM((NZ * NX, 1, 128), F32),
-            dma((5,)),
+            dma((8,)),
             dma((ROUNDS,)), dma((ROUNDS,)),
             dma((ROUNDS,)), dma((ROUNDS + 1,)),
             dma, dma((3,)),
@@ -583,7 +588,8 @@
             collective_id=0, has_side_effects=True, vmem_limit_bytes=60 * 2**20
         ),
     )(
-        queries[0], keys[0], values[0], tokens_in[0], out_weight.T, pool_keys.T, proj_weight, captions, valid_frames
+        queries[0], keys[0], values[0], tokens_in[0], out_weight.T, pool_keys.T, proj_weight, captions,
+        valid_frames.reshape(1, 1),
     )
     return block_out[None], loss[0, 0:1]
 

time: 102 us -> 100 us (0.980)
  Pallas kernels: 96.7 us -> 94.9 us
    pallas_call x1, Pallas kernels: 96.7 us -> 94.9 us  [local(): pl.pallas_call(body, out_shape=(pltpu.VMEM((TOK, D), BF16), pltpu.VMEM((1...]
where the time goes in v4:
time: 100 us; the launch traced here: 98.5 us
  Pallas kernels  94.9 us (95%)
  between operations  2.45 us (2%)
  local copies, waits for them, and re-layouts  1.17 us (1%)
    pallas_call x1, Pallas kernels, local(): pl.pallas_call(body, out_shape=(pltpu.VMEM((TOK, D), BF16), pltpu.VMEM((1...  94.9 us

profile of v4, /device:TPU:4, one launch (start us, length us, event | category | flops | bytes accessed | tf_op | source)
XLA Modules:
  0.0 98.5 jit_solution(17491508262518934207)
XLA Ops:
  1.3 94.9 %shard_map.104 = (bf16[256,3200]{1,0:T(8,128)(2,1)S(1)}, f32[1,128]{1,0:T(1,128)S(1)}) custom-call(bf16[256,3072]{1,0:T(8,128)(2,1)} %bitcast.14, bf16[256,3072]{1,0:T(8,128)(2,1)} %bitcast.15, bf16[256,3072]{1,0:T(8,128)(2,1)} %bitcast.16, bf16[256,3200]{1,0:T(8,128)(2,1)} %bitcast.13, bf16[100,3072]{1,0:T(8,128)(2,1)} %bitcast.17, ...), custom_call_target="tpu_custom_call" | custom-call | tf_op jit(solution)/shard_map/pallas_call | solution.py:537
  96.2 1.2 %copy.13 = bf16[1,256,3200]{2,1,0:T(8,128)(2,1)} copy(bf16[1,256,3200]{2,1,0:T(8,128)(2,1)S(1)} %bitcast.11) | data formatting | bytes 3276800

commit v5 on v4

--- a/solution.py
+++ b/solution.py
@@ -38,7 +38,7 @@
 def body(
     q_hbm, k_hbm, v_hbm, tok_hbm, w_hbm, pk_hbm, proj_hbm, cap_hbm, valid_hbm,
     out_ref, loss_out,
-    tok, wown, proj, pool, cap, count, blk, loss, own_a, own_x, stage_a, stage_x, m32, wt, qkv, k2, vext, osend, orecv, acc,
+    tok, wown, proj, pool, cap, count, blk, loss, own_a, own_x, stage_a, stage_x, m32, wt, qkv, k2, vlive, osend, orecv, acc,
     msg, pout, parts, emb, embs, caps, logit,
     lsem, qs, qr, os_, or_, as_, ar, x1s, x1r, z1s, z1r, z2s, z2r, x2s, x2r, x2f, sbs, sbr,
     cs, cr, ms, mr, es, er, gs, gr,
@@ -239,18 +239,18 @@
             hi = kk.astype(BF16)
             k2[rows, 0:HD] = hi
             k2[rows, HD : 2 * HD] = (kk - hi.astype(F32)).astype(BF16)
-            vext[rows, 0:HD] = jnp.where(live, qkv[r, 1, rows, :].astype(F32), 0.0).astype(BF16)
-            vext[rows, HD : 2 * HD] = jnp.where(live, 1.0, 0.0).astype(BF16)
-
-    def attend(r, start, stop):
+            vlive[rows, :] = jnp.where(live, qkv[r, 1, rows, :].astype(F32), 0.0).astype(BF16)
+
+    def attend(r, start, stop, dead):
         for i in range(start, stop):
             b = lax.rem(f + 1 + i, NF)
             qq = qkv[r, 2, pl.ds(pl.multiple_of(b * TOK, TOK), TOK), :]
             scores = nt_dot(jnp.concatenate([qq, qq], axis=1), k2[...])
             peak = jnp.max(scores, axis=1, keepdims=True)
-            weights = jnp.exp2(scores - peak).astype(BF16)
-            both = jnp.dot(weights, vext[...], preferred_element_type=F32)
-            osend[r, b] = (both[:, 0:HD] / both[:, HD : 2 * HD]).astype(BF16)
+            expo = jnp.exp2(scores - peak)
+            total = jnp.sum(expo, axis=1, keepdims=True) - dead * expo[:, 0:1]
+            weights = (expo * (1.0 / total)).astype(BF16)
+            osend[r, b] = jnp.dot(weights, vlive[...], preferred_element_type=F32).astype(BF16)
 
     def give_back(r, start, stop):
         group = r + start // 4
@@ -329,6 +329,7 @@
     loads[2].wait()
     loads[5].wait()
     valid = count[...]
+    dead = (SEQ - TPF * valid).astype(F32)
     for n in range(8):
         emb[0, n : n + 1, :] = cap[0:1, 128 * n : 128 * (n + 1)]
     own_cap = emb[0]
@@ -362,13 +363,13 @@
 
     qkv_wait(0)
     prepare(0, valid)
-    attend(0, 0, 2)
+    attend(0, 0, 2, dead)
     z2_step(0, 4)
     z2_step(1, 4)
     z1_step(0, 1)
-    attend(0, 2, 6)
+    attend(0, 2, 6, dead)
     z1_step(1, 1)
-    attend(0, 6, 8)
+    attend(0, 6, 8, dead)
     for o in range(0, 3):
         x2_forward(0, o)
     z1_step(0, 2)
@@ -377,11 +378,11 @@
 
     qkv_wait(1)
     prepare(1, valid)
-    attend(1, 0, 2)
+    attend(1, 0, 2, dead)
     z1_step(1, 2)
     sib_start(1)
     sib_start(5)
-    attend(1, 2, 5)
+    attend(1, 2, 5, dead)
     z1_step(0, 3)
     x2_forward(0, 6)
     x2_forward(0, 7)
@@ -391,7 +392,7 @@
     for o in range(0, 4):
         x2_forward(1, o)
     give_back(0, 0, 8)
-    attend(1, 5, 8)
+    attend(1, 5, 8, dead)
     give_back(1, 0, 8)
     z1_step(1, 3)
     for o in range(4, 8):
@@ -402,14 +403,14 @@
 
     qkv_wait(2)
     prepare(2, valid)
-    attend(2, 0, 4)
+    attend(2, 0, 4, dead)
     give_back(2, 0, 4)
     x2_far(0)
     sib_start(4)
     z1_step(0, 4)
     z1_step(1, 4)
     sib_start(0)
-    attend(2, 4, 8)
+    attend(2, 4, 8, dead)
     give_back(2, 4, 8)
 
     loads[1].wait()
@@ -559,7 +560,7 @@
             pltpu.VMEM((D, HEADS * HD), BF16),
             pltpu.VMEM((ROUNDS, 3, SEQ, HD), BF16),
             pltpu.VMEM((SEQ, 2 * HD), BF16),
-            pltpu.VMEM((SEQ, 2 * HD), BF16),
+            pltpu.VMEM((SEQ, HD), BF16),
             pltpu.VMEM((ROUNDS, NF, TOK, HD), BF16),
             pltpu.VMEM((TOK, HEADS * HD), BF16),
             pltpu.VMEM((TOK, D), F32),

time: 100 us -> 100 us (level)
  no operation moved by 1% of the time
where the time goes in v5:
time: 100 us; the launch traced here: 98.5 us
  Pallas kernels  94.9 us (95%)
  between operations  2.45 us (2%)
  local copies, waits for them, and re-layouts  1.17 us (1%)
    pallas_call x1, Pallas kernels, local(): pl.pallas_call(body, out_shape=(pltpu.VMEM((TOK, D), BF16), pltpu.VMEM((1...  94.9 us

profile of v5, /device:TPU:4, one launch (start us, length us, event | category | flops | bytes accessed | tf_op | source)
XLA Modules:
  0.0 98.5 jit_solution(18063613429105847214)
XLA Ops:
  1.3 94.9 %shard_map.104 = (bf16[256,3200]{1,0:T(8,128)(2,1)S(1)}, f32[1,128]{1,0:T(1,128)S(1)}) custom-call(bf16[256,3072]{1,0:T(8,128)(2,1)} %bitcast.14, bf16[256,3072]{1,0:T(8,128)(2,1)} %bitcast.15, bf16[256,3072]{1,0:T(8,128)(2,1)} %bitcast.16, bf16[256,3200]{1,0:T(8,128)(2,1)} %bitcast.13, bf16[100,3072]{1,0:T(8,128)(2,1)} %bitcast.17, ...), custom_call_target="tpu_custom_call" | custom-call | tf_op jit(solution)/shard_map/pallas_call | solution.py:538
  96.2 1.2 %copy.13 = bf16[1,256,3200]{2,1,0:T(8,128)(2,1)} copy(bf16[1,256,3200]{2,1,0:T(8,128)(2,1)S(1)} %bitcast.11) | data formatting | bytes 3276800
